TPU v7x, 512 devices: a whole 4x8x8 slice. The times are simulated.
512 devices in a mesh: seq: 64 (over y, z), head: 8 (over x, core).
Axes of the slice: x: 4, y: 8, z: 8, core: 2. Of those that a mesh axis runs over, the one named last changes fastest.
Arguments:
- hidden_state: bfloat16 [4, 8192], P(None, 'seq'), may hold values from -70 to 70
- attn_gain: bfloat16 [8192], P('seq'), may hold values from 0.099609375 to 1.8984375
- query_key_value_weight: bfloat16 [8192, 10240], P('seq', 'head'), may hold values from -0.0625 to 0.0625
- key_page_cache: bfloat16 [1024, 128, 1024], P('seq', None, 'head'), may hold values from -200 to 200
- value_page_cache: bfloat16 [1024, 128, 1024], P('seq', None, 'head'), may hold values from -11 to 11
- page_table: int32 [4, 256], replicated, may hold values from 0 to 1023, as said below
- lengths: int32 [4], replicated, may hold values from 1 to 32767, as said below
- out_weight: bfloat16 [8192, 8192], P('head', 'seq'), may hold values from -0.0625 to 0.0625
- ffn_gain: bfloat16 [8192], P('seq'), may hold values from 0.099609375 to 1.8984375
- gate_weight: bfloat16 [8192, 28672], P('seq', 'head'), may hold values from -0.0625 to 0.0625
- up_weight: bfloat16 [8192, 28672], P('seq', 'head'), may hold values from -0.0625 to 0.0625
- down_weight: bfloat16 [28672, 8192], P('head', 'seq'), may hold values from -0.03125 to 0.03125
Outputs:
- attended: bfloat16 [4, 8192], P(None, 'seq')
- mixed: bfloat16 [4, 8192], P(None, 'seq')
Inputs may be any that keep to these rules, and one draw needn't show every extreme that they name: `page_table`: entry [b, j] is the pool page holding positions j * 128 to (j + 1) * 128 - 1 of request b. Request b's pages are owned in turn: page j by (o_b + j) modulo the seq axis's size, for some o_b, so each seq device holds 4 pages of every request. Every pool page appears exactly once in the table. The new token of request b sits at position lengths[b]; in every draw one request has exactly 32767 cached tokens.
All inputs are finite; a program needn't handle non-finite values.
Results may differ from a plain program's by a relative error of at most 0.007.
Values may be sent and summed in bfloat16 or wider, within the bound.
A program may use at most 64 MiB of HBM per device.

v0:
```python
import math

import jax
import jax.numpy as jnp
from jax import lax
from jax.sharding import PartitionSpec as P

MODEL_WIDTH = 8192
QUERY_HEADS = 64
KEY_VALUE_HEADS = 8
HEAD_SIZE = 128
PAGE_TOKENS = 128


epsilon = 1e-05
rope_base = 500000.0
neg_fill = -1e30
scale_factor = 8.0
low_factor = 1.0
high_factor = 4.0
native_window = 8192.0


def combined_all(value, axis, join):
    pieces = jax.tree.map(lambda part: lax.all_gather(part, axis), value)
    head = jax.tree.map(lambda part: part[0], pieces)
    tail = jax.tree.map(lambda part: part[1:], pieces)
    total, _ = lax.scan(lambda total, section: (join(total, section), None), head, tail)
    return total


def product(form, left, right):
    return jnp.einsum(form, left, right, preferred_element_type=jnp.float32)


def rotate(vectors, position):
    half_width = vectors.shape[-1] // 2
    base_freq = rope_base ** (-jnp.arange(half_width, dtype=jnp.float32) * 2.0 / vectors.shape[-1])
    ratio = native_window * base_freq / (2.0 * math.pi)
    smooth = jnp.clip((ratio - low_factor) / (high_factor - low_factor), 0.0, 1.0)
    frequency = (1.0 - smooth) * base_freq / scale_factor + smooth * base_freq
    angles = position[..., None].astype(jnp.float32) * frequency
    cos_part = jnp.cos(angles)
    sine_part = jnp.sin(angles)
    earlier = vectors[..., :half_width]
    latter = vectors[..., half_width:]
    return jnp.concatenate(
        [earlier * cos_part - latter * sine_part, latter * cos_part + earlier * sine_part], axis=-1
    )


def owner_partial(
    key_rows, value_rows, queries, new_key, new_value, page_table, lengths, new_owner, owner
):
    slot_count, page_len = (key_rows.shape[0], key_rows.shape[1])
    requests, kv_heads, query_group, head_dim = queries.shape
    score_scale = 1.0 / math.sqrt(head_dim)
    slot_ids = owner * slot_count + jnp.arange(slot_count, dtype=jnp.int32)
    matches = page_table[None, :, :] == slot_ids[:, None, None]
    page_index = jnp.arange(page_table.shape[1], dtype=jnp.int32)
    slot_page = jnp.sum(jnp.where(matches, page_index[None, None, :], 0), axis=(1, 2))
    owned_by = jnp.any(matches, axis=2)
    slot_len = jnp.sum(jnp.where(owned_by, lengths[None, :], 0), axis=1)
    positions = slot_page[:, None] * page_len + jnp.arange(page_len, dtype=jnp.int32)[None, :]
    live_key = positions < slot_len[:, None]
    slot_query = jnp.sum(
        jnp.where(owned_by[:, :, None, None, None], queries[None], jnp.zeros((), queries.dtype)),
        axis=1,
    )
    key_heads = key_rows.reshape(slot_count, page_len, kv_heads, head_dim)
    value_heads = value_rows.reshape(slot_count, page_len, kv_heads, head_dim)
    scores = product("shgd,sthd->shgt", slot_query, key_heads) * score_scale
    masked = jnp.where(live_key[:, None, None, :], scores, neg_fill)
    slot_peak = jnp.max(masked, axis=3)
    req_peak = jnp.max(jnp.where(owned_by[:, :, None, None], slot_peak[:, None], neg_fill), axis=0)
    is_mine = new_owner == owner
    new_score = (
        jnp.sum(queries.astype(jnp.float32) * new_key.astype(jnp.float32)[:, :, None, :], axis=3)
        * score_scale
    )
    peak_score = jnp.maximum(req_peak, jnp.where(is_mine[:, None, None], new_score, neg_fill))
    slot_best = jnp.sum(jnp.where(owned_by[:, :, None, None], peak_score[None], 0.0), axis=1)
    weights = jnp.where(live_key[:, None, None, :], jnp.exp(masked - slot_best[..., None]), 0.0)
    slot_totals = jnp.sum(weights, axis=3)
    slot_accum = product("shgt,sthd->shgd", weights.astype(jnp.bfloat16), value_heads)
    totals = jnp.sum(jnp.where(owned_by[:, :, None, None], slot_totals[:, None], 0.0), axis=0)
    accum = jnp.sum(jnp.where(owned_by[:, :, None, None, None], slot_accum[:, None], 0.0), axis=0)
    new_weight = jnp.where(is_mine[:, None, None], jnp.exp(new_score - peak_score), 0.0)
    totals = totals + new_weight
    accum = (
        accum
        + new_weight.astype(jnp.bfloat16).astype(jnp.float32)[..., None]
        * new_value.astype(jnp.float32)[:, :, None, :]
    )
    return (peak_score, totals, accum)


def combine(earlier, latter):
    peak_score = jnp.maximum(earlier[0], latter[0])
    left_factor = jnp.exp(earlier[0] - peak_score)
    right_factor = jnp.exp(latter[0] - peak_score)
    totals = earlier[1] * left_factor + latter[1] * right_factor
    accum = earlier[2] * left_factor[..., None] + latter[2] * right_factor[..., None]
    return (peak_score, totals, accum)


def on_device(
    hidden_state,
    attn_gain,
    query_key_value_weight,
    key_page_cache,
    value_page_cache,
    page_table,
    lengths,
    out_weight,
    ffn_gain,
    gate_weight,
    up_weight,
    down_weight,
):
    requests = hidden_state.shape[0]
    query_group = QUERY_HEADS // KEY_VALUE_HEADS
    kv_heads = key_page_cache.shape[2] // HEAD_SIZE
    owner = lax.axis_index("seq")
    stream = hidden_state.astype(jnp.float32)
    scaled = (stream * attn_gain.astype(jnp.float32)).astype(jnp.bfloat16)
    partial_qkv = jnp.dot(scaled, query_key_value_weight, preferred_element_type=jnp.float32)
    square, combined_sum = lax.psum((jnp.sum(stream * stream, axis=1), partial_qkv), "seq")
    inv_rms = lax.rsqrt(square / MODEL_WIDTH + epsilon)
    combined_sum = (combined_sum * inv_rms[:, None]).reshape(
        requests, kv_heads, query_group + 2, HEAD_SIZE
    )
    queries = rotate(combined_sum[:, :, :query_group], lengths[:, None, None]).astype(jnp.bfloat16)
    new_key = rotate(combined_sum[:, :, query_group], lengths[:, None]).astype(jnp.bfloat16)
    new_value = combined_sum[:, :, query_group + 1].astype(jnp.bfloat16)
    new_page = jnp.take_along_axis(page_table, (lengths // PAGE_TOKENS)[:, None], axis=1)[:, 0]
    new_owner = new_page // key_page_cache.shape[0]
    peak_score, totals, accum = owner_partial(
        key_page_cache,
        value_page_cache,
        queries,
        new_key,
        new_value,
        page_table,
        lengths,
        new_owner,
        owner,
    )
    peak_score, totals, accum = combined_all((peak_score, totals, accum), "seq", combine)
    attention = (accum / totals[..., None]).astype(jnp.bfloat16).reshape(requests, -1)
    projected = lax.psum(jnp.dot(attention, out_weight, preferred_element_type=jnp.float32), "head")
    attended = (stream + projected).astype(jnp.bfloat16)
    after = attended.astype(jnp.float32)
    ffn_scaled = (after * ffn_gain.astype(jnp.float32)).astype(jnp.bfloat16)
    gate_part = jnp.dot(ffn_scaled, gate_weight, preferred_element_type=jnp.float32)
    up_part = jnp.dot(ffn_scaled, up_weight, preferred_element_type=jnp.float32)
    square_part = jnp.sum(after * after, axis=1)
    square_two, gate_sum, up_sum = lax.psum((square_part, gate_part, up_part), "seq")
    inv_norm = lax.rsqrt(square_two / MODEL_WIDTH + epsilon)
    hidden = (jax.nn.silu(gate_sum * inv_norm[:, None]) * (up_sum * inv_norm[:, None])).astype(
        jnp.bfloat16
    )
    down_part = jnp.dot(hidden, down_weight, preferred_element_type=jnp.float32)
    down_sum = lax.psum(down_part, "head")
    mixed = (after + down_sum).astype(jnp.bfloat16)
    return (attended, mixed)


def solution(mesh):
    in_specs = (
        P(None, "seq"),
        P("seq"),
        P("seq", "head"),
        P("seq", None, "head"),
        P("seq", None, "head"),
        P(),
        P(),
        P("head", "seq"),
        P("seq"),
        P("seq", "head"),
        P("seq", "head"),
        P("head", "seq"),
    )
    out_specs = (P(None, "seq"), P(None, "seq"))
    return jax.shard_map(
        on_device, mesh=mesh, in_specs=in_specs, out_specs=out_specs, check_vma=False
    )
```

profile of v0, /device:TPU:1, one launch (start us, length us, event | category | flops | bytes accessed | tf_op | source)
XLA Modules:
  0.0 588.2 jit_solution(17847963997125727010)
XLA Ops:
  7.3 0.7 copy-done.1
  8.0 0.2 compare_reduce_fusion
  8.2 0.2 fusion.6
  8.4 0.6 copy-done.11
  9.3 0.6 copy-done.12
  9.8 0.7 copy-done.9
  10.6 1.2 fusion.44
  11.8 232.1 %all-reduce.1 = (f32[4,1280]{1,0:T(4,128)S(1)}, f32[4]{0:T(128)S(1)}) all-reduce(f32[4,1280]{1,0:T(4,128)S(1)} %fusion.44, f32[4]{0:T(128)S(1)} %fusion.34), channel_id=1, replica_groups=mesh['seq'=64,'head'=8] {'seq'}, use_global_device_ids=true, to_apply=%region_3.4 | all-reduce | flops 5124 | bytes 40992 | tf_op jit(solution)/shard_map/psum | solution.py:128
  244.0 0.6 gather_fusion
  245.2 0.2 multiply_reduce_fusion
  245.6 0.5 fusion.57
  246.4 0.3 fusion.11
  246.7 0.1 select_reduce_fusion
  246.9 0.7 fusion.20
  247.6 0.6 copy-done.13
  248.2 0.2 fusion.10
  248.7 35.6 %all_gather.13 = f32[64,4,1,8]{3,1,2,0:T(4,128)S(1)} all-gather(f32[1,4,1,8]{3,1,2,0:T(4,128)S(1)} %get-tuple-element.92), channel_id=1, replica_groups=mesh['seq'=64,'head'=8] {'seq'}, dimensions={0}, use_global_device_ids=true | all-gather | bytes 8320 | tf_op jit(solution)/shard_map/all_gather | solution.py:25
  284.2 36.4 %all_gather.12 = f32[64,4,1,8]{3,1,2,0:T(4,128)S(1)} all-gather(f32[1,4,1,8]{3,1,2,0:T(4,128)S(1)} %get-tuple-element.93), channel_id=1, replica_groups=mesh['seq'=64,'head'=8] {'seq'}, dimensions={0}, use_global_device_ids=true | all-gather | bytes 8320 | tf_op jit(solution)/shard_map/all_gather | solution.py:25
  320.6 0.6 copy-done.6
  321.2 52.3 %all-gather.2.cloned.1.call-done = f32[64,4,1,8,128]{4,3,2,1,0:T(8,128)} async-done(((f32[1,4,1,8,128]{4,3,2,1,0:T(8,128)}), f32[64,4,1,8,128]{4,3,2,1,0:T(8,128)}) %all-gather.2.cloned.1.call-update) | async-done | bytes 1048592 | tf_op jit(solution)/shard_map/all_gather | solution.py:25
  373.5 0.7 slice_bitcast_fusion.1
  374.2 1.3 slice_bitcast_fusion
  375.6 7.9 %while.14 = (s32[]{:T(128)}, f32[4,1,8]{2,0,1:T(4,128)S(1)}, f32[4,1,8]{2,0,1:T(4,128)S(1)}, f32[4,1,8,128]{3,2,1,0:T(8,128)S(1)}, f32[63,4,1,8]{3,1,2,0:T(4,128...) while((s32[]{:T(128)}, f32[4,1,8]{2,0,1:T(4,128)S(1)}, ...), condition=%wide.region_15.16_spmd, body=%wide.region_14.15_spmd.sunk | while | flops 12514 | bytes 51177 | solution.py:28
  383.7 37.5 %psum.51 = f32[4,128]{1,0:T(4,128)S(1)} all-reduce(f32[4,128]{1,0:T(4,128)S(1)} %fusion.21), channel_id=1, replica_groups=mesh['seq'=64,'head'=8] {'head'}, use_global_device_ids=true, to_apply=%region_16.17 | all-reduce | flops 512 | bytes 4096 | tf_op jit(solution)/shard_map/psum | solution.py:151
  421.3 0.6 fusion.37
  421.9 0.8 fusion.49
  422.7 0.8 fusion.51
  423.6 138.8 %all-reduce.4.cloned.1.call-done = (f32[4,3584]{1,0:T(4,128)}, f32[4,3584]{1,0:T(4,128)}, f32[4]{0:T(128)}) async-done(((f32[4,3584]{1,0:T(4,128)}, f32[4,3584]{1,0:T(4,128)}, f32[4]{0:T(128)}), (f32[4,3584]{1,0:T(4,128)}, f32[4,3584]{1,0:T(4,128)}, f32[4]{0:T(128)})) %all-reduce.4.cloned.1.call-update) | async-done | bytes 114720 | tf_op jit(solution)/shard_map/psum | solution.py:158
  562.4 0.7 copy-done.14
  563.1 1.1 fusion.16
  564.2 16.6 %psum.55 = f32[4,128]{1,0:T(4,128)S(1)} all-reduce(f32[4,128]{1,0:T(4,128)S(1)} %fusion.16), channel_id=1, replica_groups=mesh['seq'=64,'head'=8] {'head'}, use_global_device_ids=true, to_apply=%region_21.22 | all-reduce | flops 512 | bytes 4096 | tf_op jit(solution)/shard_map/psum | solution.py:164
  580.8 0.6 fusion.38
  (321 shorter events, 9.4 us)
Async XLA Ops:
  7.2 414.7 %copy-start = (bf16[128,3584]{1,0:T(8,128)(2,1)S(1)}, bf16[128,3584]{1,0:T(8,128)(2,1)}, u32[]{:S(2)}) copy-start(bf16[128,3584]{1,0:T(8,128)(2,1)} %param.24) | copy-start | bytes 2752516
  7.2 366.3 %all-gather.2.cloned.1.call-start = ((), (), s32[]{:S(2)}) async-start(), calls=%async_computation | async-start | bytes 1064960 | tf_op jit(solution)/shard_map/all_gather | solution.py:25
  7.2 0.8 copy-start.1
  8.4 0.7 copy-start.11
  9.2 0.7 copy-start.12
  9.8 0.7 copy-start.9
  10.6 234.9 %copy-start.3 = (bf16[16,128,128]{2,1,0:T(8,128)(2,1)S(1)}, bf16[16,128,128]{2,1,0:T(8,128)(2,1)}, u32[]{:S(2)}) copy-start(bf16[16,128,128]{2,1,0:T(8,128)(2,1)} %param.17) | copy-start | bytes 1572868
  244.7 1.7 copy-start.4
  247.6 0.7 copy-start.13
  247.6 314.8 %all-reduce.4.cloned.1.call-start = ((), (), s32[]{:S(2)}) async-start(), calls=%async_computation.1 | async-start | bytes 230400 | tf_op jit(solution)/shard_map/psum | solution.py:158
  284.2 36.4 %copy-start.5 = (f32[64,4,1,8]{3,1,2,0:T(4,128)}, f32[64,4,1,8]{3,1,2,0:T(4,128)S(1)}, u32[]{:S(2)}) copy-start(f32[64,4,1,8]{3,1,2,0:T(4,128)S(1)} %all_gather.13) | copy-start | bytes 24580
  320.6 0.6 copy-start.6
  374.2 1.4 slice-start
  374.2 1.4 slice-start.1
  374.2 9.4 %copy-start.7 = (bf16[1024,128]{1,0:T(8,128)(2,1)S(1)}, bf16[1024,128]{1,0:T(8,128)(2,1)}, u32[]{:S(2)}) copy-start(bf16[1024,128]{1,0:T(8,128)(2,1)} %param.21) | copy-start | bytes 786436
  375.6 47.2 %copy-start.2 = (bf16[128,3584]{1,0:T(8,128)(2,1)S(1)}, bf16[128,3584]{1,0:T(8,128)(2,1)}, u32[]{:S(2)}) copy-start(bf16[128,3584]{1,0:T(8,128)(2,1)} %param.23) | copy-start | bytes 2752516
  421.9 158.9 %copy-start.8 = (bf16[4,128]{1,0:T(4,128)(2,1)}, bf16[4,128]{1,0:T(4,128)(2,1)S(1)}, u32[]{:S(2)}) copy-start(bf16[4,128]{1,0:T(4,128)(2,1)S(1)} %get-tuple-element.85) | copy-start | bytes 3076
  421.9 141.2 %copy-start.10 = (bf16[3584,128]{1,0:T(8,128)(2,1)S(1)}, bf16[3584,128]{1,0:T(8,128)(2,1)}, u32[]{:S(2)}) copy-start(bf16[3584,128]{1,0:T(8,128)(2,1)} %param.25) | copy-start | bytes 2752516
  562.4 0.7 copy-start.14
Sparse Core Ops, SparseCore 0:
  247.7 125.7 all-gather.1
  423.7 138.6 all-reduce.3
where the time goes:
time: 589 us; the launch traced here: 588 us
  blocking collectives  358 us (61%)
  waiting for transfers between devices  191 us (32%)
  between operations  14.3 us (2%)
  other arithmetic  11.3 us (2%)
  local copies, waits for them, and re-layouts  7.76 us (1%)
    psum x1, blocking collectives, on_device(): lax.psum((jnp.sum(stream * stream, axis=1), partial_qkv), 'seq')  232 us
    psum x1, waiting for transfers between devices, on_device(): lax.psum((square_part, gate_part, up_part), 'seq')  139 us
    all_gather x2, blocking collectives, combined_all(): pieces = jax.tree.map(lambda part: lax.all_gather(part, axis), value)  71.9 us
    all_gather x1, waiting for transfers between devices, combined_all(): pieces = jax.tree.map(lambda part: lax.all_gather(part, axis), value)  52.3 us
    psum x1, blocking collectives, on_device(): lax.psum(jnp.dot(attention, out_weight, preferred_element_type=jnp.float3...  37.5 us
    psum x1, blocking collectives, on_device(): down_sum = lax.psum(down_part, 'head')  16.6 us
  transfers between devices with their start and end apart: 2, of which 2 were waited for; matrix products, arithmetic and copies ran while one was open for 0% of the time, Pallas kernels for 0%

commit v1 on v0

v1 whole, which is shorter than its diff:
```python
import functools
import math

import jax
import jax.numpy as jnp
import numpy as np
from jax import lax
from jax.experimental import pallas as pl
from jax.experimental.pallas import tpu as pltpu
from jax.sharding import PartitionSpec as P

MODEL_WIDTH = 8192
QUERY_HEADS = 64
KEY_VALUE_HEADS = 8
HEAD_SIZE = 128
PAGE_TOKENS = 128
REQUESTS = 4
GROUP = QUERY_HEADS // KEY_VALUE_HEADS
ROWS = GROUP * REQUESTS
SLOTS = 16
LANES = 128
SIDE = 8
HEADS = 8
TILES = 28
HALF_TILES = 14

epsilon = 1e-05
neg_fill = -1e30
MESH = pl.DeviceIdType.MESH
f32 = jnp.float32
bf16 = jnp.bfloat16

RING_ORDER = (4, 3, 5, 2, 6, 1, 7)


def rope_frequencies():
    index = np.arange(HEAD_SIZE // 2, dtype=np.float64)
    base = 500000.0 ** (-2.0 * index / HEAD_SIZE)
    ratio = 8192.0 * base / (2.0 * math.pi)
    smooth = np.clip((ratio - 1.0) / 3.0, 0.0, 1.0)
    frequency = (1.0 - smooth) * base / 8.0 + smooth * base
    return np.concatenate([frequency, frequency]).astype(np.float32)[None, :]


def layer(
    len_ref,
    freq_ref,
    hidden_any,
    gain_any,
    wqkv_any,
    keys_any,
    values_any,
    table_any,
    wout_any,
    fgain_any,
    wgate_any,
    wup_any,
    wdown_any,
    attended_ref,
    mixed_ref,
    hidden,
    gain,
    wqkv,
    keys,
    values,
    table,
    wout,
    fgain,
    wgate,
    wup,
    wdown,
    load_sem,
    qkv_out1,
    qkv_in1,
    qkv_out2,
    qkv_in2,
    live_buf,
    part_out1,
    part_in1,
    part_out2,
    part_in2,
    proj_buf,
    gate_rows,
    up_rows,
    chunk_out,
    chunk_in,
    piece_out,
    piece_in,
    act_buf,
    act_rows,
    down_buf,
    send_sem,
    recv_sem,
):
    seq = lax.axis_index("seq")
    head = lax.axis_index("head")
    core = lax.rem(head, 2)
    row_y = seq // SIDE
    row_z = lax.rem(seq, SIDE)
    first = row_y + core * (row_z - row_y)
    second = row_z + core * (row_y - row_z)

    def seq_of(one, two):
        return one * (SIDE - (SIDE - 1) * core) + two * (1 + (SIDE - 1) * core)

    def first_peer(d):
        other = lax.rem(first + d, SIDE)
        return other, (seq_of(other, second), head)

    def second_peer(d):
        other = lax.rem(second + d, SIDE)
        return other, (seq_of(first, other), head)

    def head_peer(d):
        other = lax.rem(head + d, HEADS)
        return other, (seq, other)

    barrier = pltpu.get_barrier_semaphore()
    for d in range(1, 8):
        for peer in (first_peer, second_peer, head_peer):
            pl.semaphore_signal(barrier, inc=1, device_id=peer(d)[1], device_id_type=MESH)

    loads = {}
    for i, (name, src, dst) in enumerate(
        (
            ("hidden", hidden_any, hidden),
            ("gain", gain_any, gain),
            ("wqkv", wqkv_any, wqkv),
            ("table", table_any, table),
            ("keys", keys_any, keys),
            ("values", values_any, values),
            ("wout", wout_any, wout),
            ("fgain", fgain_any, fgain),
            ("wgate", wgate_any, wgate),
            ("wup", wup_any, wup),
            ("wdown", wdown_any, wdown),
        )
    ):
        loads[name] = pltpu.make_async_copy(src, dst, load_sem.at[i])
        loads[name].start()

    started = []

    def exchange(step, peer, src_of, dst_of):
        copies = []
        for d in RING_ORDER:
            other, device = peer(d)
            copy = pltpu.make_async_remote_copy(
                src_ref=src_of(other),
                dst_ref=dst_of(d),
                send_sem=send_sem.at[step, d - 1],
                recv_sem=recv_sem.at[step, d - 1],
                device_id=device,
                device_id_type=MESH,
            )
            copy.start()
            copies.append(copy)
        started.extend(copies)
        return copies

    def arrive(copies):
        for copy in copies:
            copy.wait_recv()

    loads["hidden"].wait()
    loads["gain"].wait()
    stream = hidden[...].astype(f32)
    scaled = (stream * gain[...].astype(f32)).astype(bf16)
    square = jnp.broadcast_to(jnp.sum(stream * stream, axis=1, keepdims=True), (REQUESTS, LANES))
    loads["wqkv"].wait()
    part = jnp.dot(scaled, wqkv[...], preferred_element_type=f32)
    part_rows = jnp.concatenate(
        [part[:, t * LANES : (t + 1) * LANES] for t in range(GROUP + 2)]
        + [square, jnp.zeros((REQUESTS, LANES), f32)],
        axis=0,
    )
    qkv_out1[...] = part_rows.astype(bf16)

    pl.semaphore_wait(barrier, 21)
    copies = exchange(0, first_peer, lambda o: qkv_out1, lambda d: qkv_in1.at[d - 1])

    sub = lax.broadcasted_iota(jnp.int32, (8, 1), 0)
    request = lax.rem(sub, REQUESTS)
    length = jnp.zeros((8, 1), jnp.int32)
    for b in range(REQUESTS):
        length = jnp.where(request == b, len_ref[b], length)
    loads["table"].wait()
    pages = table[...]
    pages = jnp.concatenate([pages, pages], axis=0)
    page_count = pages.shape[1]
    page_index = lax.broadcasted_iota(jnp.int32, (8, page_count), 1)
    lane = lax.broadcasted_iota(jnp.int32, (8, LANES), 1)
    for j in range(SLOTS):
        hit = jnp.sum(
            jnp.where(pages == seq * SLOTS + j, (page_index + 1).astype(f32), 0.0), axis=1, keepdims=True
        ).astype(jnp.int32)
        limit = jnp.where(hit > 0, length - (hit - 1) * PAGE_TOKENS, 0)
        live_buf[:, j * LANES : (j + 1) * LANES] = jnp.where(lane < limit, 1.0, 0.0)
    mine_page = (page_index == length // PAGE_TOKENS) & (pages >= seq * SLOTS) & (pages < (seq + 1) * SLOTS)
    mine = jnp.sum(jnp.where(mine_page, 1.0, 0.0), axis=1, keepdims=True) > 0.5
    angle = length.astype(f32) * freq_ref[...]
    cos_part = jnp.cos(angle)
    sine_part = jnp.where(lane < HEAD_SIZE // 2, -jnp.sin(angle), jnp.sin(angle))

    arrive(copies)
    total = part_rows
    for d in range(7):
        total = total + qkv_in1[d].astype(f32)
    qkv_out2[...] = total.astype(bf16)
    copies = exchange(1, second_peer, lambda o: qkv_out2, lambda d: qkv_in2.at[d - 1])
    loads["keys"].wait()
    loads["values"].wait()
    arrive(copies)
    for d in range(7):
        total = total + qkv_in2[d].astype(f32)

    square_all = total[40:44]
    square_all = jnp.concatenate([square_all, square_all], axis=0)
    inv_rms = lax.rsqrt(square_all / MODEL_WIDTH + epsilon)
    joined = total[0:40].reshape(5, 8, LANES) * inv_rms
    swapped = pltpu.roll(joined.reshape(40, LANES), HEAD_SIZE // 2, 1).reshape(5, 8, LANES)
    turned = joined * cos_part + swapped * sine_part
    queries = turned[0:4].reshape(ROWS, LANES).astype(bf16)
    new_key = turned[4][0:4].astype(bf16).astype(f32)
    new_key = jnp.concatenate([new_key, new_key], axis=0)
    new_value = joined[4][4:8].astype(bf16).astype(f32)
    new_value = jnp.concatenate([new_value, new_value], axis=0)

    scale = 1.0 / math.sqrt(HEAD_SIZE)
    tokens = SLOTS * PAGE_TOKENS
    scores = lax.dot_general(
        queries,
        keys[...].reshape(tokens, HEAD_SIZE),
        (((1,), (1,)), ((), ())),
        preferred_element_type=f32,
    )
    live = live_buf[...] > 0.5
    masked = jnp.where(live, scores.reshape(4, 8, tokens) * scale, neg_fill)
    new_score = (
        jnp.sum(queries.astype(f32).reshape(4, 8, LANES) * new_key, axis=2, keepdims=True) * scale
    )
    peak = jnp.maximum(
        jnp.max(masked, axis=2, keepdims=True), jnp.where(mine, new_score, neg_fill)
    )
    weight = jnp.where(live, jnp.exp(masked - peak), 0.0)
    new_weight = jnp.where(mine, jnp.exp(new_score - peak), 0.0)
    denom = jnp.sum(weight, axis=2, keepdims=True) + new_weight
    accum = jnp.dot(
        weight.reshape(ROWS, tokens).astype(bf16),
        values[...].reshape(tokens, HEAD_SIZE),
        preferred_element_type=f32,
    ).reshape(4, 8, LANES)
    accum = accum + new_weight.astype(bf16).astype(f32) * new_value
    some = denom > 0.0
    safe = jnp.where(some, denom, 1.0)
    mean = (accum / safe).reshape(ROWS, LANES)
    lse = jnp.where(some, peak + jnp.log(safe), neg_fill).reshape(ROWS, 1)

    diagonal = lax.broadcasted_iota(jnp.int32, (ROWS, LANES), 0) == lax.broadcasted_iota(
        jnp.int32, (ROWS, LANES), 1
    )
    lse_row = jnp.sum(jnp.where(diagonal, lse, 0.0), axis=0, keepdims=True)
    stat_row = lax.broadcasted_iota(jnp.int32, (16, LANES), 0)

    def packed(mean, lse_row):
        high = lse_row.astype(bf16).astype(f32)
        rest = lse_row - high
        middle = rest.astype(bf16).astype(f32)
        low = rest - middle
        stats = jnp.where(
            stat_row == 0, high, jnp.where(stat_row == 1, middle, jnp.where(stat_row == 2, low, 0.0))
        )
        return jnp.concatenate([mean, stats], axis=0).astype(bf16)

    def merged(mean, lse_row, arrived):
        means, lses = [mean], [lse_row]
        for d in range(7):
            block = arrived[d].astype(f32)
            means.append(block[0:ROWS])
            lses.append(block[ROWS : ROWS + 1] + block[ROWS + 1 : ROWS + 2] + block[ROWS + 2 : ROWS + 3])
        best = functools.reduce(jnp.maximum, lses)
        factors = [jnp.exp(part - best) for part in lses]
        whole = functools.reduce(jnp.add, factors)
        result = None
        for factor, part in zip(factors, means):
            column = jnp.sum(jnp.where(diagonal, factor / whole, 0.0), axis=1, keepdims=True)
            result = column * part if result is None else result + column * part
        return result, best + jnp.log(whole)

    part_out1[...] = packed(mean, lse_row)
    copies = exchange(2, first_peer, lambda o: part_out1, lambda d: part_in1.at[d - 1])
    loads["wout"].wait()
    loads["fgain"].wait()
    arrive(copies)
    mean, lse_row = merged(mean, lse_row, part_in1)
    part_out2[...] = packed(mean, lse_row)
    copies = exchange(3, second_peer, lambda o: part_out2, lambda d: part_in2.at[d - 1])
    loads["wgate"].wait()
    loads["wup"].wait()
    loads["wdown"].wait()
    arrive(copies)
    mean, _ = merged(mean, lse_row, part_in2)

    attention = jnp.concatenate(
        [mean[g * REQUESTS : (g + 1) * REQUESTS] for g in range(GROUP)], axis=1
    ).astype(bf16)
    proj_buf[head] = jnp.dot(attention, wout[...], preferred_element_type=f32)
    copies = exchange(4, head_peer, lambda o: proj_buf.at[head], lambda d: proj_buf.at[head])
    arrive(copies)
    projected = proj_buf[0]
    for h in range(1, HEADS):
        projected = projected + proj_buf[h]
    attended = (stream + projected).astype(bf16)
    attended_ref[...] = attended
    after = attended.astype(f32)
    ffn = (after * fgain[...].astype(f32)).astype(bf16).astype(f32)
    ffn = jnp.concatenate([ffn, ffn], axis=0).astype(bf16)
    square = jnp.sum(after * after, axis=1, keepdims=True)
    gate_part = jnp.dot(ffn, wgate[...], preferred_element_type=f32)
    up_part = jnp.dot(ffn, wup[...], preferred_element_type=f32)
    for t in range(TILES):
        gate_rows[t * 8 : (t + 1) * 8, :] = gate_part[:, t * LANES : (t + 1) * LANES]
        up_rows[t * 8 : (t + 1) * 8, :] = up_part[:, t * LANES : (t + 1) * LANES]
    blank = jnp.zeros((2, LANES), f32)
    blank_row = lax.broadcasted_iota(jnp.int32, (2, LANES), 0)
    for c in range(SIDE):
        b, half = c // 2, c % 2
        span = pl.ds(half * HALF_TILES * 8 + b, HALF_TILES, stride=8)
        tail = jnp.where(blank_row == 0, square[b : b + 1], 0.0)
        chunk_out[c] = jnp.concatenate([gate_rows[span, :], tail, up_rows[span, :], blank], axis=0).astype(bf16)
    copies = exchange(5, first_peer, lambda o: chunk_out.at[o], lambda d: chunk_in.at[d - 1])
    own = chunk_out[first].astype(f32)
    arrive(copies)
    for d in range(7):
        own = own + chunk_in[d].astype(f32)
    piece_out[...] = own.astype(bf16)
    copies = exchange(6, second_peer, lambda o: piece_out, lambda d: piece_in.at[d - 1])
    arrive(copies)
    for d in range(7):
        own = own + piece_in[d].astype(f32)
    inv_norm = lax.rsqrt(own[HALF_TILES : HALF_TILES + 1] / MODEL_WIDTH + epsilon)
    gate = own[0:16] * inv_norm
    act = gate / (1.0 + jnp.exp(-gate)) * (own[16:32] * inv_norm)
    act_buf[first] = act.astype(bf16)
    copies = exchange(7, first_peer, lambda o: act_buf.at[first], lambda d: act_buf.at[first])
    arrive(copies)
    act_rows[...] = act_buf[...].reshape(SIDE * 16, LANES).astype(f32)
    units = jnp.concatenate(
        [
            act_rows[pl.ds((t // HALF_TILES) * 16 + t % HALF_TILES, REQUESTS, stride=32), :]
            for t in range(TILES)
        ],
        axis=1,
    ).astype(bf16)
    down_buf[head] = jnp.dot(units, wdown[...], preferred_element_type=f32)
    copies = exchange(8, head_peer, lambda o: down_buf.at[head], lambda d: down_buf.at[head])
    arrive(copies)
    down = down_buf[0]
    for h in range(1, HEADS):
        down = down + down_buf[h]
    mixed_ref[...] = (after + down).astype(bf16)

    for copy in started:
        copy.wait_send()


def on_device(
    hidden_state,
    attn_gain,
    query_key_value_weight,
    key_page_cache,
    value_page_cache,
    page_table,
    lengths,
    out_weight,
    ffn_gain,
    gate_weight,
    up_weight,
    down_weight,
):
    requests, width = hidden_state.shape
    arrays = (
        hidden_state,
        attn_gain.reshape(1, width),
        query_key_value_weight,
        key_page_cache,
        value_page_cache,
        page_table,
        out_weight,
        ffn_gain.reshape(1, width),
        gate_weight,
        up_weight,
        down_weight,
    )
    any_spec = pl.BlockSpec(memory_space=pl.ANY)
    vmem_spec = pl.BlockSpec(memory_space=pltpu.VMEM)
    out = jax.ShapeDtypeStruct((requests, width), bf16)
    rows = 48
    return pl.pallas_call(
        layer,
        out_shape=(out, out),
        in_specs=[pl.BlockSpec(memory_space=pltpu.SMEM), vmem_spec] + [any_spec] * len(arrays),
        out_specs=(vmem_spec, vmem_spec),
        scratch_shapes=[pltpu.VMEM(a.shape, a.dtype) for a in arrays]
        + [
            pltpu.SemaphoreType.DMA((len(arrays),)),
            pltpu.VMEM((rows, LANES), bf16),
            pltpu.VMEM((7, rows, LANES), bf16),
            pltpu.VMEM((rows, LANES), bf16),
            pltpu.VMEM((7, rows, LANES), bf16),
            pltpu.VMEM((8, SLOTS * PAGE_TOKENS), f32),
            pltpu.VMEM((rows, LANES), bf16),
            pltpu.VMEM((7, rows, LANES), bf16),
            pltpu.VMEM((rows, LANES), bf16),
            pltpu.VMEM((7, rows, LANES), bf16),
            pltpu.VMEM((HEADS, REQUESTS, LANES), f32),
            pltpu.VMEM((TILES * 8, LANES), f32),
            pltpu.VMEM((TILES * 8, LANES), f32),
            pltpu.VMEM((SIDE, 32, LANES), bf16),
            pltpu.VMEM((7, 32, LANES), bf16),
            pltpu.VMEM((32, LANES), bf16),
            pltpu.VMEM((7, 32, LANES), bf16),
            pltpu.VMEM((SIDE, 16, LANES), bf16),
            pltpu.VMEM((SIDE * 16, LANES), f32),
            pltpu.VMEM((HEADS, REQUESTS, LANES), f32),
            pltpu.SemaphoreType.DMA((9, 7)),
            pltpu.SemaphoreType.DMA((9, 7)),
        ],
        compiler_params=pltpu.CompilerParams(
            collective_id=0, has_side_effects=True, vmem_limit_bytes=48 * 1024 * 1024
        ),
    )(lengths, jnp.asarray(rope_frequencies()), *arrays)


def solution(mesh):
    in_specs = (
        P(None, "seq"),
        P("seq"),
        P("seq", "head"),
        P("seq", None, "head"),
        P("seq", None, "head"),
        P(),
        P(),
        P("head", "seq"),
        P("seq"),
        P("seq", "head"),
        P("seq", "head"),
        P("head", "seq"),
    )
    out_specs = (P(None, "seq"), P(None, "seq"))
    return jax.shard_map(
        on_device, mesh=mesh, in_specs=in_specs, out_specs=out_specs, check_vma=False
    )
```

time: 589 us -> 70.1 us (0.12)
  blocking collectives: 358 us -> 0 us
  waiting for transfers between devices: 191 us -> 0 us
  Pallas kernels: 0 us -> 58.9 us
  between operations: 14.3 us -> 0.69 us
  other arithmetic: 11.3 us -> 0 us
    psum x3 -> x0, blocking collectives: 286 us -> none  [the longest x1 232 us: on_device(): lax.psum((jnp.sum(stream * stream, axis=1), partial_qkv), 'seq')]
    psum x1 -> x0, waiting for transfers between devices: 139 us -> none  [on_device(): lax.psum((square_part, gate_part, up_part), 'seq')]
    all_gather x2 -> x0, blocking collectives: 71.9 us -> none  [combined_all(): pieces = jax.tree.map(lambda part: lax.all_gather(part, axis), value)]
    pallas_call x0 -> x1, Pallas kernels: none -> 58.9 us  [on_device(): pl.pallas_call(layer, out_shape=(out, out), in_specs=[pl.BlockSpec(memory...]
    all_gather x1 -> x0, waiting for transfers between devices: 52.3 us -> none  [combined_all(): pieces = jax.tree.map(lambda part: lax.all_gather(part, axis), value)]
    add x67 -> x0, other arithmetic: 5.91 us -> none  [the longest x63 5.14 us: combine(): earlier[2] * left_factor[..., None] + latter[2] * right_factor[..., None]]
  transfers between devices with their start and end apart: 2 -> 0, of which waited for: 2 -> 0; matrix products, arithmetic and copies ran while one was open for 0% -> 0% of each run, Pallas kernels for 0% -> 0%
where the time goes in v1:
time: 70.1 us; the launch traced here: 69.6 us
  Pallas kernels  58.9 us (84%)
  local copies, waits for them, and re-layouts  10 us (14%)
    pallas_call x1, Pallas kernels, on_device(): pl.pallas_call(layer, out_shape=(out, out), in_specs=[pl.BlockSpec(memory...  58.9 us
    unnamed x28, local copies, waits for them, and re-layouts  10 us

profile of v1, /device:TPU:1, one launch (start us, length us, event | category | flops | bytes accessed | tf_op | source)
XLA Modules:
  0.0 69.6 jit_solution(4953803184534185281)
XLA Ops:
  0.6 0.0 copy-start.10
  0.6 0.0 copy-start.11
  0.7 0.0 copy-start.12
  0.7 0.0 copy-start.8
  0.7 0.0 copy-start.9
  0.7 0.6 copy-done.10
  1.3 0.0 copy-done.11
  1.3 0.0 copy-done.12
  1.3 0.0 copy-done.8
  1.4 0.0 copy-done.9
  1.4 0.0 copy-start
  1.4 1.2 %copy-done = bf16[128,3584]{1,0:T(8,128)(2,1)S(1)} copy-done((bf16[128,3584]{1,0:T(8,128)(2,1)S(1)}, bf16[128,3584]{1,0:T(8,128)(2,1)}, u32[]{:S(2)}) %copy-start) | copy-done | bytes 917528
  2.5 0.0 copy-start.1
  2.5 1.2 %copy-done.1 = bf16[128,3584]{1,0:T(8,128)(2,1)S(1)} copy-done((bf16[128,3584]{1,0:T(8,128)(2,1)S(1)}, bf16[128,3584]{1,0:T(8,128)(2,1)}, u32[]{:S(2)}) %copy-start.1) | copy-done | bytes 917528
  3.7 0.0 copy-start.2
  3.7 1.2 %copy-done.2 = bf16[3584,128]{1,0:T(8,128)(2,1)S(1)} copy-done((bf16[3584,128]{1,0:T(8,128)(2,1)S(1)}, bf16[3584,128]{1,0:T(8,128)(2,1)}, u32[]{:S(2)}) %copy-start.2) | copy-done | bytes 917528
  4.9 0.0 copy-start.3
  4.9 1.0 %copy-done.3 = bf16[16,128,128]{2,1,0:T(8,128)(2,1)S(1)} copy-done((bf16[16,128,128]{2,1,0:T(8,128)(2,1)S(1)}, bf16[16,128,128]{2,1,0:T(8,128)(2,1)}, u32[]{:S(2)}) %copy-start.3) | copy-done | bytes 524312
  5.9 0.0 copy-start.4
  5.9 1.0 %copy-done.4 = bf16[16,128,128]{2,1,0:T(8,128)(2,1)S(1)} copy-done((bf16[16,128,128]{2,1,0:T(8,128)(2,1)S(1)}, bf16[16,128,128]{2,1,0:T(8,128)(2,1)}, u32[]{:S(2)}) %copy-start.4) | copy-done | bytes 524312
  7.0 0.0 copy-start.5
  7.0 1.0 %copy-done.5 = bf16[128,1280]{1,0:T(8,128)(2,1)S(1)} copy-done((bf16[128,1280]{1,0:T(8,128)(2,1)S(1)}, bf16[128,1280]{1,0:T(8,128)(2,1)}, u32[]{:S(2)}) %copy-start.5) | copy-done | bytes 327704
  8.0 0.0 copy-start.6
  8.0 0.9 %copy-done.6 = bf16[1024,128]{1,0:T(8,128)(2,1)S(1)} copy-done((bf16[1024,128]{1,0:T(8,128)(2,1)S(1)}, bf16[1024,128]{1,0:T(8,128)(2,1)}, u32[]{:S(2)}) %copy-start.6) | copy-done | bytes 262168
  8.9 0.0 copy-start.7
  8.9 0.7 copy-done.7
  9.6 58.9 %shard_map.140 = (bf16[4,128]{1,0:T(4,128)(2,1)S(1)}, bf16[4,128]{1,0:T(4,128)(2,1)S(1)}) custom-call(s32[4]{0:T(128)S(1)} %copy-done.9, f32[1,128]{1,0:T(1,128)S(1)} %copy-done.12, bf16[4,128]{1,0:T(4,128)(2,1)S(1)} %copy-done.8, bf16[1,128]{1,0:T(2,128)(2,1)S(1)} %bitcast.2, bf16[128,1280]{1,0:T(8,128)(2,1)S(1)} %copy-done.5, ...), custom_call_target="tpu_custom_call" | custom-call | tf_op jit(solution)/shard_map/pallas_call | solution.py:399
  68.5 0.6 copy.17
  69.1 0.6 copy.18
Async XLA Ops:
  0.6 0.7 copy-start.10
  0.6 0.7 copy-start.11
  0.7 0.7 copy-start.12
  0.7 0.7 copy-start.8
  0.7 0.7 copy-start.9
  1.4 1.2 %copy-start = (bf16[128,3584]{1,0:T(8,128)(2,1)S(1)}, bf16[128,3584]{1,0:T(8,128)(2,1)}, u32[]{:S(2)}) copy-start(bf16[128,3584]{1,0:T(8,128)(2,1)} %wgate_any.1) | copy-start | bytes 2752516
  2.5 1.2 %copy-start.1 = (bf16[128,3584]{1,0:T(8,128)(2,1)S(1)}, bf16[128,3584]{1,0:T(8,128)(2,1)}, u32[]{:S(2)}) copy-start(bf16[128,3584]{1,0:T(8,128)(2,1)} %wup_any.1) | copy-start | bytes 2752516
  3.7 1.2 %copy-start.2 = (bf16[3584,128]{1,0:T(8,128)(2,1)S(1)}, bf16[3584,128]{1,0:T(8,128)(2,1)}, u32[]{:S(2)}) copy-start(bf16[3584,128]{1,0:T(8,128)(2,1)} %wdown_any.1) | copy-start | bytes 2752516
  4.9 1.0 %copy-start.3 = (bf16[16,128,128]{2,1,0:T(8,128)(2,1)S(1)}, bf16[16,128,128]{2,1,0:T(8,128)(2,1)}, u32[]{:S(2)}) copy-start(bf16[16,128,128]{2,1,0:T(8,128)(2,1)} %keys_any.1) | copy-start | bytes 1572868
  5.9 1.0 %copy-start.4 = (bf16[16,128,128]{2,1,0:T(8,128)(2,1)S(1)}, bf16[16,128,128]{2,1,0:T(8,128)(2,1)}, u32[]{:S(2)}) copy-start(bf16[16,128,128]{2,1,0:T(8,128)(2,1)} %values_any.1) | copy-start | bytes 1572868
  7.0 1.0 %copy-start.5 = (bf16[128,1280]{1,0:T(8,128)(2,1)S(1)}, bf16[128,1280]{1,0:T(8,128)(2,1)}, u32[]{:S(2)}) copy-start(bf16[128,1280]{1,0:T(8,128)(2,1)} %wqkv_any.1) | copy-start | bytes 983044
  8.0 0.9 %copy-start.6 = (bf16[1024,128]{1,0:T(8,128)(2,1)S(1)}, bf16[1024,128]{1,0:T(8,128)(2,1)}, u32[]{:S(2)}) copy-start(bf16[1024,128]{1,0:T(8,128)(2,1)} %wout_any.1) | copy-start | bytes 786436
  8.9 0.7 copy-start.7

commit v2 on v1

--- a/solution.py
+++ b/solution.py
@@ -43,8 +43,6 @@
 
 
 def layer(
-    len_ref,
-    freq_ref,
     hidden_any,
     gain_any,
     wqkv_any,
@@ -56,8 +54,9 @@
     wgate_any,
     wup_any,
     wdown_any,
-    attended_ref,
-    mixed_ref,
+    len_any,
+    freq_any,
+    both_ref,
     hidden,
     gain,
     wqkv,
@@ -69,6 +68,8 @@
     wgate,
     wup,
     wdown,
+    len_ref,
+    freq_ref,
     load_sem,
     qkv_out1,
     qkv_in1,
@@ -115,52 +116,51 @@
         other = lax.rem(head + d, HEADS)
         return other, (seq, other)
 
+    loads = {}
+
+    def load(index, name, src, dst):
+        loads[name] = pltpu.make_async_copy(src, dst, load_sem.at[index])
+        loads[name].start()
+
+    load(0, "hidden", hidden_any, hidden)
+    load(1, "gain", gain_any, gain)
+    load(2, "wqkv", wqkv_any, wqkv)
+
     barrier = pltpu.get_barrier_semaphore()
-    for d in range(1, 8):
+    for d in RING_ORDER:
         for peer in (first_peer, second_peer, head_peer):
             pl.semaphore_signal(barrier, inc=1, device_id=peer(d)[1], device_id_type=MESH)
 
-    loads = {}
-    for i, (name, src, dst) in enumerate(
-        (
-            ("hidden", hidden_any, hidden),
-            ("gain", gain_any, gain),
-            ("wqkv", wqkv_any, wqkv),
-            ("table", table_any, table),
-            ("keys", keys_any, keys),
-            ("values", values_any, values),
-            ("wout", wout_any, wout),
-            ("fgain", fgain_any, fgain),
-            ("wgate", wgate_any, wgate),
-            ("wup", wup_any, wup),
-            ("wdown", wdown_any, wdown),
-        )
-    ):
-        loads[name] = pltpu.make_async_copy(src, dst, load_sem.at[i])
-        loads[name].start()
-
-    started = []
+    load(3, "table", table_any, table)
+    load(4, "lengths", len_any, len_ref)
+    load(5, "freq", freq_any, freq_ref)
+    load(6, "keys", keys_any, keys)
+    load(7, "values", values_any, values)
+    load(8, "wout", wout_any, wout)
+    load(9, "fgain", fgain_any, fgain)
+    load(10, "wgate", wgate_any, wgate)
+    load(11, "wup", wup_any, wup)
+    load(12, "wdown", wdown_any, wdown)
 
     def exchange(step, peer, src_of, dst_of):
-        copies = []
         for d in RING_ORDER:
             other, device = peer(d)
-            copy = pltpu.make_async_remote_copy(
+            pltpu.make_async_remote_copy(
                 src_ref=src_of(other),
                 dst_ref=dst_of(d),
-                send_sem=send_sem.at[step, d - 1],
-                recv_sem=recv_sem.at[step, d - 1],
+                send_sem=send_sem.at[step],
+                recv_sem=recv_sem.at[step],
                 device_id=device,
                 device_id_type=MESH,
-            )
-            copy.start()
-            copies.append(copy)
-        started.extend(copies)
-        return copies
-
-    def arrive(copies):
-        for copy in copies:
-            copy.wait_recv()
+            ).start()
+
+    def arrive(step, blocks):
+        seven = blocks.at[pl.ds(0, 7)]
+        pltpu.make_async_copy(seven, seven, recv_sem.at[step]).wait()
+
+    def departed(step, blocks):
+        seven = blocks.at[pl.ds(0, 7)]
+        pltpu.make_async_copy(seven, seven, send_sem.at[step]).wait()
 
     loads["hidden"].wait()
     loads["gain"].wait()
@@ -177,11 +177,12 @@
     qkv_out1[...] = part_rows.astype(bf16)
 
     pl.semaphore_wait(barrier, 21)
-    copies = exchange(0, first_peer, lambda o: qkv_out1, lambda d: qkv_in1.at[d - 1])
+    exchange(0, first_peer, lambda o: qkv_out1, lambda d: qkv_in1.at[d - 1])
 
     sub = lax.broadcasted_iota(jnp.int32, (8, 1), 0)
     request = lax.rem(sub, REQUESTS)
     length = jnp.zeros((8, 1), jnp.int32)
+    loads["lengths"].wait()
     for b in range(REQUESTS):
         length = jnp.where(request == b, len_ref[b], length)
     loads["table"].wait()
@@ -198,19 +199,21 @@
         live_buf[:, j * LANES : (j + 1) * LANES] = jnp.where(lane < limit, 1.0, 0.0)
     mine_page = (page_index == length // PAGE_TOKENS) & (pages >= seq * SLOTS) & (pages < (seq + 1) * SLOTS)
     mine = jnp.sum(jnp.where(mine_page, 1.0, 0.0), axis=1, keepdims=True) > 0.5
-    angle = length.astype(f32) * freq_ref[...]
-    cos_part = jnp.cos(angle)
-    sine_part = jnp.where(lane < HEAD_SIZE // 2, -jnp.sin(angle), jnp.sin(angle))
-
-    arrive(copies)
+
+    arrive(0, qkv_in1)
     total = part_rows
     for d in range(7):
         total = total + qkv_in1[d].astype(f32)
     qkv_out2[...] = total.astype(bf16)
-    copies = exchange(1, second_peer, lambda o: qkv_out2, lambda d: qkv_in2.at[d - 1])
+    exchange(1, second_peer, lambda o: qkv_out2, lambda d: qkv_in2.at[d - 1])
+    loads["freq"].wait()
+    angle = length.astype(f32) * freq_ref[...]
+    cos_part = jnp.cos(angle)
+    sine_part = jnp.sin(angle)
+    sine_part = jnp.where(lane < HEAD_SIZE // 2, -sine_part, sine_part)
     loads["keys"].wait()
     loads["values"].wait()
-    arrive(copies)
+    arrive(1, qkv_in2)
     for d in range(7):
         total = total + qkv_in2[d].astype(f32)
 
@@ -288,30 +291,29 @@
         return result, best + jnp.log(whole)
 
     part_out1[...] = packed(mean, lse_row)
-    copies = exchange(2, first_peer, lambda o: part_out1, lambda d: part_in1.at[d - 1])
+    exchange(2, first_peer, lambda o: part_out1, lambda d: part_in1.at[d - 1])
     loads["wout"].wait()
     loads["fgain"].wait()
-    arrive(copies)
+    arrive(2, part_in1)
     mean, lse_row = merged(mean, lse_row, part_in1)
     part_out2[...] = packed(mean, lse_row)
-    copies = exchange(3, second_peer, lambda o: part_out2, lambda d: part_in2.at[d - 1])
+    exchange(3, second_peer, lambda o: part_out2, lambda d: part_in2.at[d - 1])
     loads["wgate"].wait()
     loads["wup"].wait()
     loads["wdown"].wait()
-    arrive(copies)
+    arrive(3, part_in2)
     mean, _ = merged(mean, lse_row, part_in2)
 
     attention = jnp.concatenate(
         [mean[g * REQUESTS : (g + 1) * REQUESTS] for g in range(GROUP)], axis=1
     ).astype(bf16)
     proj_buf[head] = jnp.dot(attention, wout[...], preferred_element_type=f32)
-    copies = exchange(4, head_peer, lambda o: proj_buf.at[head], lambda d: proj_buf.at[head])
-    arrive(copies)
+    exchange(4, head_peer, lambda o: proj_buf.at[head], lambda d: proj_buf.at[head])
+    arrive(4, proj_buf)
     projected = proj_buf[0]
     for h in range(1, HEADS):
         projected = projected + proj_buf[h]
     attended = (stream + projected).astype(bf16)
-    attended_ref[...] = attended
     after = attended.astype(f32)
     ffn = (after * fgain[...].astype(f32)).astype(bf16).astype(f32)
     ffn = jnp.concatenate([ffn, ffn], axis=0).astype(bf16)
@@ -328,22 +330,22 @@
         span = pl.ds(half * HALF_TILES * 8 + b, HALF_TILES, stride=8)
         tail = jnp.where(blank_row == 0, square[b : b + 1], 0.0)
         chunk_out[c] = jnp.concatenate([gate_rows[span, :], tail, up_rows[span, :], blank], axis=0).astype(bf16)
-    copies = exchange(5, first_peer, lambda o: chunk_out.at[o], lambda d: chunk_in.at[d - 1])
+    exchange(5, first_peer, lambda o: chunk_out.at[o], lambda d: chunk_in.at[d - 1])
     own = chunk_out[first].astype(f32)
-    arrive(copies)
+    arrive(5, chunk_in)
     for d in range(7):
         own = own + chunk_in[d].astype(f32)
     piece_out[...] = own.astype(bf16)
-    copies = exchange(6, second_peer, lambda o: piece_out, lambda d: piece_in.at[d - 1])
-    arrive(copies)
+    exchange(6, second_peer, lambda o: piece_out, lambda d: piece_in.at[d - 1])
+    arrive(6, piece_in)
     for d in range(7):
         own = own + piece_in[d].astype(f32)
     inv_norm = lax.rsqrt(own[HALF_TILES : HALF_TILES + 1] / MODEL_WIDTH + epsilon)
     gate = own[0:16] * inv_norm
     act = gate / (1.0 + jnp.exp(-gate)) * (own[16:32] * inv_norm)
     act_buf[first] = act.astype(bf16)
-    copies = exchange(7, first_peer, lambda o: act_buf.at[first], lambda d: act_buf.at[first])
-    arrive(copies)
+    exchange(7, first_peer, lambda o: act_buf.at[first], lambda d: act_buf.at[first])
+    arrive(7, act_buf)
     act_rows[...] = act_buf[...].reshape(SIDE * 16, LANES).astype(f32)
     units = jnp.concatenate(
         [
@@ -353,15 +355,17 @@
         axis=1,
     ).astype(bf16)
     down_buf[head] = jnp.dot(units, wdown[...], preferred_element_type=f32)
-    copies = exchange(8, head_peer, lambda o: down_buf.at[head], lambda d: down_buf.at[head])
-    arrive(copies)
+    exchange(8, head_peer, lambda o: down_buf.at[head], lambda d: down_buf.at[head])
+    arrive(8, down_buf)
     down = down_buf[0]
     for h in range(1, HEADS):
         down = down + down_buf[h]
-    mixed_ref[...] = (after + down).astype(bf16)
-
-    for copy in started:
-        copy.wait_send()
+    both_ref[...] = jnp.concatenate([after, after + down], axis=0).astype(bf16)
+
+    for step, blocks in enumerate(
+        (qkv_in1, qkv_in2, part_in1, part_in2, proj_buf, chunk_in, piece_in, act_buf, down_buf)
+    ):
+        departed(step, blocks)
 
 
 def on_device(
@@ -391,17 +395,21 @@
         gate_weight,
         up_weight,
         down_weight,
-    )
-    any_spec = pl.BlockSpec(memory_space=pl.ANY)
+        lengths,
+        jnp.asarray(rope_frequencies()),
+    )
+    hbm_spec = pl.BlockSpec(memory_space=pltpu.HBM)
     vmem_spec = pl.BlockSpec(memory_space=pltpu.VMEM)
-    out = jax.ShapeDtypeStruct((requests, width), bf16)
+    out = pltpu.VMEM((2 * requests, width), bf16)
     rows = 48
-    return pl.pallas_call(
+    both = pl.pallas_call(
         layer,
-        out_shape=(out, out),
-        in_specs=[pl.BlockSpec(memory_space=pltpu.SMEM), vmem_spec] + [any_spec] * len(arrays),
-        out_specs=(vmem_spec, vmem_spec),
-        scratch_shapes=[pltpu.VMEM(a.shape, a.dtype) for a in arrays]
+        out_shape=out,
+        in_specs=[hbm_spec] * len(arrays),
+        out_specs=vmem_spec,
+        scratch_shapes=[
+            pltpu.SMEM(a.shape, a.dtype) if a is lengths else pltpu.VMEM(a.shape, a.dtype) for a in arrays
+        ]
         + [
             pltpu.SemaphoreType.DMA((len(arrays),)),
             pltpu.VMEM((rows, LANES), bf16),
@@ -423,13 +431,14 @@
             pltpu.VMEM((SIDE, 16, LANES), bf16),
             pltpu.VMEM((SIDE * 16, LANES), f32),
             pltpu.VMEM((HEADS, REQUESTS, LANES), f32),
-            pltpu.SemaphoreType.DMA((9, 7)),
-            pltpu.SemaphoreType.DMA((9, 7)),
+            pltpu.SemaphoreType.DMA((9,)),
+            pltpu.SemaphoreType.DMA((9,)),
         ],
         compiler_params=pltpu.CompilerParams(
             collective_id=0, has_side_effects=True, vmem_limit_bytes=48 * 1024 * 1024
         ),
-    )(lengths, jnp.asarray(rope_frequencies()), *arrays)
+    )(*[pltpu.with_memory_space_constraint(a, pltpu.HBM) for a in arrays])
+    return both[:requests], both[requests:]
 
 
 def solution(mesh):

time: 70.1 us -> 58 us (0.83)
  local copies, waits for them, and re-layouts: 10 us -> 0.57 us
  Pallas kernels: 58.9 us -> 56.7 us
    unnamed x28 -> x0, local copies, waits for them, and re-layouts: 10 us -> none
    pallas_call x1, Pallas kernels: 58.9 us -> 56.7 us  [on_device(): pl.pallas_call(layer, out_shape=out, in_specs=[hbm_spec] * len(arrays), o...]
where the time goes in v2:
time: 58 us; the launch traced here: 57.9 us
  Pallas kernels  56.7 us (98%)
  between operations  0.64 us (1%)
    pallas_call x1, Pallas kernels, on_device(): pl.pallas_call(layer, out_shape=out, in_specs=[hbm_spec] * len(arrays), o...  56.7 us

profile of v2, /device:TPU:1, one launch (start us, length us, event | category | flops | bytes accessed | tf_op | source)
XLA Modules:
  0.0 57.9 jit_solution(7998430097843796926)
XLA Ops:
  0.6 56.7 %shard_map.140 = bf16[8,128]{1,0:T(8,128)(2,1)S(1)} custom-call(bf16[4,128]{1,0:T(4,128)(2,1)} %hidden_any.1, bf16[1,128]{1,0:T(2,128)(2,1)} %bitcast.2, bf16[128,1280]{1,0:T(8,128)(2,1)} %wqkv_any.1, bf16[16,128,128]{2,1,0:T(8,128)(2,1)} %keys_any.1, bf16[16,128,128]{2,1,0:T(8,128)(2,1)} %values_any.1, s32[4,256]{1,0:T(4,128)} %table_any.1, ...), custom_call_target="tpu_custom_call" | custom-call | tf_op jit(solution)/shard_map/pallas_call | solution.py:405
  57.3 0.6 fusion

commit v3 on v2

--- a/solution.py
+++ b/solution.py
@@ -21,8 +21,6 @@
 LANES = 128
 SIDE = 8
 HEADS = 8
-TILES = 28
-HALF_TILES = 14
 
 epsilon = 1e-05
 neg_fill = -1e30
@@ -30,7 +28,14 @@
 f32 = jnp.float32
 bf16 = jnp.bfloat16
 
+PEERS = 7
 RING_ORDER = (4, 3, 5, 2, 6, 1, 7)
+OWNERS = 7
+CHUNK = 512
+
+
+def ring_distance(i):
+    return 4 + ((i + 1) // 2) * (1 - 2 * lax.rem(i, 2))
 
 
 def rope_frequencies():
@@ -76,22 +81,23 @@
     qkv_out2,
     qkv_in2,
     live_buf,
+    keys_turned,
     part_out1,
     part_in1,
     part_out2,
     part_in2,
     proj_buf,
-    gate_rows,
-    up_rows,
+    chunk_sum,
     chunk_out,
     chunk_in,
     piece_out,
     piece_in,
     act_buf,
-    act_rows,
+    down_sum,
     down_buf,
     send_sem,
     recv_sem,
+    act_sem,
 ):
     seq = lax.axis_index("seq")
     head = lax.axis_index("head")
@@ -127,9 +133,15 @@
     load(2, "wqkv", wqkv_any, wqkv)
 
     barrier = pltpu.get_barrier_semaphore()
-    for d in RING_ORDER:
-        for peer in (first_peer, second_peer, head_peer):
-            pl.semaphore_signal(barrier, inc=1, device_id=peer(d)[1], device_id_type=MESH)
+
+    @pl.loop(0, PEERS)
+    def announce(i):
+        pl.semaphore_signal(barrier, inc=1, device_id=first_peer(i + 1)[1], device_id_type=MESH)
+
+    @pl.loop(0, PEERS)
+    def announce_more(i):
+        for peer in (second_peer, head_peer):
+            pl.semaphore_signal(barrier, inc=1, device_id=peer(i + 1)[1], device_id_type=MESH)
 
     load(3, "table", table_any, table)
     load(4, "lengths", len_any, len_ref)
@@ -143,7 +155,9 @@
     load(12, "wdown", wdown_any, wdown)
 
     def exchange(step, peer, src_of, dst_of):
-        for d in RING_ORDER:
+        @pl.loop(0, PEERS)
+        def send(i):
+            d = ring_distance(i)
             other, device = peer(d)
             pltpu.make_async_remote_copy(
                 src_ref=src_of(other),
@@ -155,12 +169,12 @@
             ).start()
 
     def arrive(step, blocks):
-        seven = blocks.at[pl.ds(0, 7)]
-        pltpu.make_async_copy(seven, seven, recv_sem.at[step]).wait()
-
-    def departed(step, blocks):
-        seven = blocks.at[pl.ds(0, 7)]
-        pltpu.make_async_copy(seven, seven, send_sem.at[step]).wait()
+        some = blocks.at[pl.ds(0, PEERS)]
+        pltpu.make_async_copy(some, some, recv_sem.at[step]).wait()
+
+    def departed(step, blocks, count=PEERS):
+        some = blocks.at[pl.ds(0, count)]
+        pltpu.make_async_copy(some, some, send_sem.at[step]).wait()
 
     loads["hidden"].wait()
     loads["gain"].wait()
@@ -199,6 +213,11 @@
         live_buf[:, j * LANES : (j + 1) * LANES] = jnp.where(lane < limit, 1.0, 0.0)
     mine_page = (page_index == length // PAGE_TOKENS) & (pages >= seq * SLOTS) & (pages < (seq + 1) * SLOTS)
     mine = jnp.sum(jnp.where(mine_page, 1.0, 0.0), axis=1, keepdims=True) > 0.5
+    loads["freq"].wait()
+    angle = length.astype(f32) * freq_ref[...]
+    cos_part = jnp.cos(angle)
+    sine_part = jnp.sin(angle)
+    sine_part = jnp.where(lane < HEAD_SIZE // 2, -sine_part, sine_part)
 
     arrive(0, qkv_in1)
     total = part_rows
@@ -206,13 +225,17 @@
         total = total + qkv_in1[d].astype(f32)
     qkv_out2[...] = total.astype(bf16)
     exchange(1, second_peer, lambda o: qkv_out2, lambda d: qkv_in2.at[d - 1])
-    loads["freq"].wait()
-    angle = length.astype(f32) * freq_ref[...]
-    cos_part = jnp.cos(angle)
-    sine_part = jnp.sin(angle)
-    sine_part = jnp.where(lane < HEAD_SIZE // 2, -sine_part, sine_part)
     loads["keys"].wait()
+
+    @pl.loop(0, SLOTS // 4)
+    def turn(step):
+        for k in range(4):
+            j = step * 4 + k
+            span = pl.ds(pl.multiple_of(j * PAGE_TOKENS, PAGE_TOKENS), PAGE_TOKENS)
+            keys_turned[:, span] = keys[j].T
+
     loads["values"].wait()
+    departed(0, qkv_in1)
     arrive(1, qkv_in2)
     for d in range(7):
         total = total + qkv_in2[d].astype(f32)
@@ -231,12 +254,7 @@
 
     scale = 1.0 / math.sqrt(HEAD_SIZE)
     tokens = SLOTS * PAGE_TOKENS
-    scores = lax.dot_general(
-        queries,
-        keys[...].reshape(tokens, HEAD_SIZE),
-        (((1,), (1,)), ((), ())),
-        preferred_element_type=f32,
-    )
+    scores = jnp.dot(queries, keys_turned[...], preferred_element_type=f32)
     live = live_buf[...] > 0.5
     masked = jnp.where(live, scores.reshape(4, 8, tokens) * scale, neg_fill)
     new_score = (
@@ -294,6 +312,7 @@
     exchange(2, first_peer, lambda o: part_out1, lambda d: part_in1.at[d - 1])
     loads["wout"].wait()
     loads["fgain"].wait()
+    departed(1, qkv_in2)
     arrive(2, part_in1)
     mean, lse_row = merged(mean, lse_row, part_in1)
     part_out2[...] = packed(mean, lse_row)
@@ -301,6 +320,7 @@
     loads["wgate"].wait()
     loads["wup"].wait()
     loads["wdown"].wait()
+    departed(2, part_in1)
     arrive(3, part_in2)
     mean, _ = merged(mean, lse_row, part_in2)
 
@@ -309,63 +329,105 @@
     ).astype(bf16)
     proj_buf[head] = jnp.dot(attention, wout[...], preferred_element_type=f32)
     exchange(4, head_peer, lambda o: proj_buf.at[head], lambda d: proj_buf.at[head])
+    departed(3, part_in2)
     arrive(4, proj_buf)
     projected = proj_buf[0]
     for h in range(1, HEADS):
         projected = projected + proj_buf[h]
     attended = (stream + projected).astype(bf16)
     after = attended.astype(f32)
-    ffn = (after * fgain[...].astype(f32)).astype(bf16).astype(f32)
-    ffn = jnp.concatenate([ffn, ffn], axis=0).astype(bf16)
-    square = jnp.sum(after * after, axis=1, keepdims=True)
-    gate_part = jnp.dot(ffn, wgate[...], preferred_element_type=f32)
-    up_part = jnp.dot(ffn, wup[...], preferred_element_type=f32)
-    for t in range(TILES):
-        gate_rows[t * 8 : (t + 1) * 8, :] = gate_part[:, t * LANES : (t + 1) * LANES]
-        up_rows[t * 8 : (t + 1) * 8, :] = up_part[:, t * LANES : (t + 1) * LANES]
-    blank = jnp.zeros((2, LANES), f32)
-    blank_row = lax.broadcasted_iota(jnp.int32, (2, LANES), 0)
-    for c in range(SIDE):
-        b, half = c // 2, c % 2
-        span = pl.ds(half * HALF_TILES * 8 + b, HALF_TILES, stride=8)
-        tail = jnp.where(blank_row == 0, square[b : b + 1], 0.0)
-        chunk_out[c] = jnp.concatenate([gate_rows[span, :], tail, up_rows[span, :], blank], axis=0).astype(bf16)
-    exchange(5, first_peer, lambda o: chunk_out.at[o], lambda d: chunk_in.at[d - 1])
-    own = chunk_out[first].astype(f32)
-    arrive(5, chunk_in)
-    for d in range(7):
-        own = own + chunk_in[d].astype(f32)
-    piece_out[...] = own.astype(bf16)
-    exchange(6, second_peer, lambda o: piece_out, lambda d: piece_in.at[d - 1])
-    arrive(6, piece_in)
-    for d in range(7):
-        own = own + piece_in[d].astype(f32)
-    inv_norm = lax.rsqrt(own[HALF_TILES : HALF_TILES + 1] / MODEL_WIDTH + epsilon)
-    gate = own[0:16] * inv_norm
-    act = gate / (1.0 + jnp.exp(-gate)) * (own[16:32] * inv_norm)
-    act_buf[first] = act.astype(bf16)
-    exchange(7, first_peer, lambda o: act_buf.at[first], lambda d: act_buf.at[first])
-    arrive(7, act_buf)
-    act_rows[...] = act_buf[...].reshape(SIDE * 16, LANES).astype(f32)
-    units = jnp.concatenate(
-        [
-            act_rows[pl.ds((t // HALF_TILES) * 16 + t % HALF_TILES, REQUESTS, stride=32), :]
-            for t in range(TILES)
-        ],
-        axis=1,
-    ).astype(bf16)
-    down_buf[head] = jnp.dot(units, wdown[...], preferred_element_type=f32)
+    ffn = (after * fgain[...].astype(f32)).astype(bf16)
+    square = jnp.broadcast_to(jnp.sum(after * after, axis=1, keepdims=True), (REQUESTS, LANES))
+
+    def chunk_of(owner):
+        span = pl.ds(pl.multiple_of(owner * CHUNK, CHUNK), CHUNK)
+        gate_part = jnp.dot(ffn, wgate[:, span], preferred_element_type=f32)
+        up_part = jnp.dot(ffn, wup[:, span], preferred_element_type=f32)
+        return jnp.concatenate([gate_part, up_part, square], axis=1)
+
+    owns = first < OWNERS
+    for d in RING_ORDER:
+        other, device = first_peer(d)
+        chunk_out[d - 1] = chunk_of(jnp.minimum(other, OWNERS - 1)).astype(bf16)
+
+        @pl.when(other < OWNERS)
+        def send_chunk():
+            pltpu.make_async_remote_copy(
+                src_ref=chunk_out.at[d - 1],
+                dst_ref=chunk_in.at[d - 1],
+                send_sem=send_sem.at[5],
+                recv_sem=recv_sem.at[5],
+                device_id=device,
+                device_id_type=MESH,
+            ).start()
+
+    chunk_sum[...] = chunk_of(jnp.minimum(first, OWNERS - 1))
+    down_sum[...] = jnp.zeros((REQUESTS, LANES), f32)
+    departed(4, proj_buf)
+
+    def down_of(owner):
+        span = pl.ds(pl.multiple_of(owner * CHUNK, CHUNK), CHUNK)
+        down_sum[...] += jnp.dot(act_buf[owner], wdown[span, :], preferred_element_type=f32)
+
+    @pl.when(owns)
+    def own_chunk():
+        total = chunk_sum[...]
+        arrive(5, chunk_in)
+        for d in range(PEERS):
+            total = total + chunk_in[d].astype(f32)
+        piece_out[...] = total.astype(bf16)
+        exchange(6, second_peer, lambda o: piece_out, lambda d: piece_in.at[d - 1])
+        departed(5, chunk_in, OWNERS - 1)
+        arrive(6, piece_in)
+        for d in range(PEERS):
+            total = total + piece_in[d].astype(f32)
+        inv_norm = lax.rsqrt(total[:, 2 * CHUNK : 2 * CHUNK + 1] / MODEL_WIDTH + epsilon)
+        gate = total[:, :CHUNK] * inv_norm
+        act = gate / (1.0 + jnp.exp(-gate)) * (total[:, CHUNK : 2 * CHUNK] * inv_norm)
+        act_buf[first] = act.astype(bf16)
+
+        @pl.loop(0, PEERS)
+        def send_act(i):
+            d = ring_distance(i)
+            other, device = first_peer(d)
+            pltpu.make_async_remote_copy(
+                src_ref=act_buf.at[first],
+                dst_ref=act_buf.at[first],
+                send_sem=send_sem.at[7],
+                recv_sem=act_sem.at[d - 1],
+                device_id=device,
+                device_id_type=MESH,
+            ).start()
+
+        departed(6, piece_in)
+        down_of(first)
+
+    @pl.when(jnp.logical_not(owns))
+    def no_chunk():
+        departed(5, chunk_in, OWNERS)
+
+    for d in reversed(RING_ORDER):
+        owner = lax.rem(first + SIDE - d, SIDE)
+
+        @pl.when(owner < OWNERS)
+        def take_act():
+            block = act_buf.at[owner]
+            pltpu.make_async_copy(block, block, act_sem.at[d - 1]).wait()
+            down_of(owner)
+
+    down_buf[head] = down_sum[...]
     exchange(8, head_peer, lambda o: down_buf.at[head], lambda d: down_buf.at[head])
+
+    @pl.when(owns)
+    def act_sent():
+        departed(7, act_buf)
+
     arrive(8, down_buf)
     down = down_buf[0]
     for h in range(1, HEADS):
         down = down + down_buf[h]
     both_ref[...] = jnp.concatenate([after, after + down], axis=0).astype(bf16)
-
-    for step, blocks in enumerate(
-        (qkv_in1, qkv_in2, part_in1, part_in2, proj_buf, chunk_in, piece_in, act_buf, down_buf)
-    ):
-        departed(step, blocks)
+    departed(8, down_buf)
 
 
 def on_device(
@@ -417,22 +479,23 @@
             pltpu.VMEM((rows, LANES), bf16),
             pltpu.VMEM((7, rows, LANES), bf16),
             pltpu.VMEM((8, SLOTS * PAGE_TOKENS), f32),
+            pltpu.VMEM((HEAD_SIZE, SLOTS * PAGE_TOKENS), bf16),
             pltpu.VMEM((rows, LANES), bf16),
             pltpu.VMEM((7, rows, LANES), bf16),
             pltpu.VMEM((rows, LANES), bf16),
             pltpu.VMEM((7, rows, LANES), bf16),
             pltpu.VMEM((HEADS, REQUESTS, LANES), f32),
-            pltpu.VMEM((TILES * 8, LANES), f32),
-            pltpu.VMEM((TILES * 8, LANES), f32),
-            pltpu.VMEM((SIDE, 32, LANES), bf16),
-            pltpu.VMEM((7, 32, LANES), bf16),
-            pltpu.VMEM((32, LANES), bf16),
-            pltpu.VMEM((7, 32, LANES), bf16),
-            pltpu.VMEM((SIDE, 16, LANES), bf16),
-            pltpu.VMEM((SIDE * 16, LANES), f32),
+            pltpu.VMEM((REQUESTS, 2 * CHUNK + LANES), f32),
+            pltpu.VMEM((PEERS, REQUESTS, 2 * CHUNK + LANES), bf16),
+            pltpu.VMEM((PEERS, REQUESTS, 2 * CHUNK + LANES), bf16),
+            pltpu.VMEM((REQUESTS, 2 * CHUNK + LANES), bf16),
+            pltpu.VMEM((PEERS, REQUESTS, 2 * CHUNK + LANES), bf16),
+            pltpu.VMEM((SIDE, REQUESTS, CHUNK), bf16),
+            pltpu.VMEM((REQUESTS, LANES), f32),
             pltpu.VMEM((HEADS, REQUESTS, LANES), f32),
             pltpu.SemaphoreType.DMA((9,)),
             pltpu.SemaphoreType.DMA((9,)),
+            pltpu.SemaphoreType.DMA((PEERS,)),
         ],
         compiler_params=pltpu.CompilerParams(
             collective_id=0, has_side_effects=True, vmem_limit_bytes=48 * 1024 * 1024

time: 58 us -> 58.1 us (level)
  no operation moved by 1% of the time
where the time goes in v3:
time: 58.1 us; the launch traced here: 58 us
  Pallas kernels  56.7 us (98%)
  between operations  0.64 us (1%)
    pallas_call x1, Pallas kernels, on_device(): pl.pallas_call(layer, out_shape=out, in_specs=[hbm_spec] * len(arrays), o...  56.7 us

profile of v3, /device:TPU:1, one launch (start us, length us, event | category | flops | bytes accessed | tf_op | source)
XLA Modules:
  0.0 58.0 jit_solution(53142453660494522)
XLA Ops:
  0.6 56.7 %shard_map.140 = bf16[8,128]{1,0:T(8,128)(2,1)S(1)} custom-call(bf16[4,128]{1,0:T(4,128)(2,1)} %hidden_any.1, bf16[1,128]{1,0:T(2,128)(2,1)} %bitcast.2, bf16[128,1280]{1,0:T(8,128)(2,1)} %wqkv_any.1, bf16[16,128,128]{2,1,0:T(8,128)(2,1)} %keys_any.1, bf16[16,128,128]{2,1,0:T(8,128)(2,1)} %values_any.1, s32[4,256]{1,0:T(4,128)} %table_any.1, ...), custom_call_target="tpu_custom_call" | custom-call | tf_op jit(solution)/shard_map/pallas_call | solution.py:467
  57.4 0.6 fusion

commit v4 on v3

--- a/solution.py
+++ b/solution.py
@@ -29,9 +29,8 @@
 bf16 = jnp.bfloat16
 
 PEERS = 7
-RING_ORDER = (4, 3, 5, 2, 6, 1, 7)
-OWNERS = 7
-CHUNK = 512
+OWNERS = 28
+DEVICES = 64
 
 
 def ring_distance(i):
@@ -90,14 +89,10 @@
     chunk_sum,
     chunk_out,
     chunk_in,
-    piece_out,
-    piece_in,
     act_buf,
-    down_sum,
     down_buf,
     send_sem,
     recv_sem,
-    act_sem,
 ):
     seq = lax.axis_index("seq")
     head = lax.axis_index("head")
@@ -168,8 +163,8 @@
                 device_id_type=MESH,
             ).start()
 
-    def arrive(step, blocks):
-        some = blocks.at[pl.ds(0, PEERS)]
+    def arrive(step, blocks, count=PEERS):
+        some = blocks.at[pl.ds(0, count)]
         pltpu.make_async_copy(some, some, recv_sem.at[step]).wait()
 
     def departed(step, blocks, count=PEERS):
@@ -338,96 +333,86 @@
     after = attended.astype(f32)
     ffn = (after * fgain[...].astype(f32)).astype(bf16)
     square = jnp.broadcast_to(jnp.sum(after * after, axis=1, keepdims=True), (REQUESTS, LANES))
-
-    def chunk_of(owner):
-        span = pl.ds(pl.multiple_of(owner * CHUNK, CHUNK), CHUNK)
-        gate_part = jnp.dot(ffn, wgate[:, span], preferred_element_type=f32)
-        up_part = jnp.dot(ffn, wup[:, span], preferred_element_type=f32)
-        return jnp.concatenate([gate_part, up_part, square], axis=1)
-
-    owns = first < OWNERS
-    for d in RING_ORDER:
-        other, device = first_peer(d)
-        chunk_out[d - 1] = chunk_of(jnp.minimum(other, OWNERS - 1)).astype(bf16)
-
-        @pl.when(other < OWNERS)
-        def send_chunk():
+    gate_part = jnp.dot(ffn, wgate[...], preferred_element_type=f32)
+    up_part = jnp.dot(ffn, wup[...], preferred_element_type=f32)
+    for p in range(OWNERS):
+        span = slice(p * LANES, (p + 1) * LANES)
+        chunk_out[p] = jnp.concatenate([gate_part[:, span], up_part[:, span], square], axis=1).astype(bf16)
+
+    mine_p = seq // 2
+    owns = (lax.rem(seq, 2) == core) & (mine_p < OWNERS)
+
+    @pl.loop(0, OWNERS)
+    def send_chunk(i):
+        p = lax.rem(mine_p + 1 + i, OWNERS)
+        owner = 2 * p + core
+
+        @pl.when(owner != seq)
+        def start():
             pltpu.make_async_remote_copy(
-                src_ref=chunk_out.at[d - 1],
-                dst_ref=chunk_in.at[d - 1],
+                src_ref=chunk_out.at[p],
+                dst_ref=chunk_in.at[seq],
                 send_sem=send_sem.at[5],
                 recv_sem=recv_sem.at[5],
-                device_id=device,
+                device_id=(owner, head),
                 device_id_type=MESH,
             ).start()
 
-    chunk_sum[...] = chunk_of(jnp.minimum(first, OWNERS - 1))
-    down_sum[...] = jnp.zeros((REQUESTS, LANES), f32)
     departed(4, proj_buf)
-
-    def down_of(owner):
-        span = pl.ds(pl.multiple_of(owner * CHUNK, CHUNK), CHUNK)
-        down_sum[...] += jnp.dot(act_buf[owner], wdown[span, :], preferred_element_type=f32)
 
     @pl.when(owns)
     def own_chunk():
+        chunk_in[seq] = chunk_out[mine_p]
+        arrive(5, chunk_in, DEVICES - 1)
+        chunk_sum[...] = jnp.zeros((REQUESTS, 3 * LANES), f32)
+
+        @pl.loop(0, DEVICES // 8)
+        def add(i):
+            total = chunk_sum[...]
+            for k in range(8):
+                total = total + chunk_in[i * 8 + k].astype(f32)
+            chunk_sum[...] = total
+
         total = chunk_sum[...]
-        arrive(5, chunk_in)
-        for d in range(PEERS):
-            total = total + chunk_in[d].astype(f32)
-        piece_out[...] = total.astype(bf16)
-        exchange(6, second_peer, lambda o: piece_out, lambda d: piece_in.at[d - 1])
-        departed(5, chunk_in, OWNERS - 1)
-        arrive(6, piece_in)
-        for d in range(PEERS):
-            total = total + piece_in[d].astype(f32)
-        inv_norm = lax.rsqrt(total[:, 2 * CHUNK : 2 * CHUNK + 1] / MODEL_WIDTH + epsilon)
-        gate = total[:, :CHUNK] * inv_norm
-        act = gate / (1.0 + jnp.exp(-gate)) * (total[:, CHUNK : 2 * CHUNK] * inv_norm)
-        act_buf[first] = act.astype(bf16)
-
-        @pl.loop(0, PEERS)
+        inv_norm = lax.rsqrt(total[:, 2 * LANES :] / MODEL_WIDTH + epsilon)
+        gate = total[:, :LANES] * inv_norm
+        act = gate / (1.0 + jnp.exp(-gate)) * (total[:, LANES : 2 * LANES] * inv_norm)
+        act_buf[mine_p] = act.astype(bf16)
+
+        @pl.loop(1, DEVICES)
         def send_act(i):
-            d = ring_distance(i)
-            other, device = first_peer(d)
+            other = lax.rem(seq + i, DEVICES)
             pltpu.make_async_remote_copy(
-                src_ref=act_buf.at[first],
-                dst_ref=act_buf.at[first],
-                send_sem=send_sem.at[7],
-                recv_sem=act_sem.at[d - 1],
-                device_id=device,
+                src_ref=act_buf.at[mine_p],
+                dst_ref=act_buf.at[mine_p],
+                send_sem=send_sem.at[6],
+                recv_sem=recv_sem.at[6],
+                device_id=(other, head),
                 device_id_type=MESH,
             ).start()
 
-        departed(6, piece_in)
-        down_of(first)
+        departed(5, chunk_in, OWNERS - 1)
+        arrive(6, act_buf, OWNERS - 1)
 
     @pl.when(jnp.logical_not(owns))
     def no_chunk():
         departed(5, chunk_in, OWNERS)
-
-    for d in reversed(RING_ORDER):
-        owner = lax.rem(first + SIDE - d, SIDE)
-
-        @pl.when(owner < OWNERS)
-        def take_act():
-            block = act_buf.at[owner]
-            pltpu.make_async_copy(block, block, act_sem.at[d - 1]).wait()
-            down_of(owner)
-
-    down_buf[head] = down_sum[...]
-    exchange(8, head_peer, lambda o: down_buf.at[head], lambda d: down_buf.at[head])
+        arrive(6, act_buf, OWNERS)
+
+    units = jnp.concatenate([act_buf[p] for p in range(OWNERS)], axis=1)
+    down_buf[head] = jnp.dot(units, wdown[...], preferred_element_type=f32)
+    exchange(7, head_peer, lambda o: down_buf.at[head], lambda d: down_buf.at[head])
 
     @pl.when(owns)
     def act_sent():
-        departed(7, act_buf)
-
-    arrive(8, down_buf)
+        departed(6, act_buf, DEVICES - 1)
+
+    arrive(7, down_buf)
     down = down_buf[0]
     for h in range(1, HEADS):
         down = down + down_buf[h]
     both_ref[...] = jnp.concatenate([after, after + down], axis=0).astype(bf16)
-    departed(8, down_buf)
+    departed(7, down_buf)
 
 
 def on_device(
@@ -485,17 +470,13 @@
             pltpu.VMEM((rows, LANES), bf16),
             pltpu.VMEM((7, rows, LANES), bf16),
             pltpu.VMEM((HEADS, REQUESTS, LANES), f32),
-            pltpu.VMEM((REQUESTS, 2 * CHUNK + LANES), f32),
-            pltpu.VMEM((PEERS, REQUESTS, 2 * CHUNK + LANES), bf16),
-            pltpu.VMEM((PEERS, REQUESTS, 2 * CHUNK + LANES), bf16),
-            pltpu.VMEM((REQUESTS, 2 * CHUNK + LANES), bf16),
-            pltpu.VMEM((PEERS, REQUESTS, 2 * CHUNK + LANES), bf16),
-            pltpu.VMEM((SIDE, REQUESTS, CHUNK), bf16),
-            pltpu.VMEM((REQUESTS, LANES), f32),
+            pltpu.VMEM((REQUESTS, 3 * LANES), f32),
+            pltpu.VMEM((OWNERS, REQUESTS, 3 * LANES), bf16),
+            pltpu.VMEM((DEVICES, REQUESTS, 3 * LANES), bf16),
+            pltpu.VMEM((DEVICES, REQUESTS, LANES), bf16),
             pltpu.VMEM((HEADS, REQUESTS, LANES), f32),
-            pltpu.SemaphoreType.DMA((9,)),
-            pltpu.SemaphoreType.DMA((9,)),
-            pltpu.SemaphoreType.DMA((PEERS,)),
+            pltpu.SemaphoreType.DMA((8,)),
+            pltpu.SemaphoreType.DMA((8,)),
         ],
         compiler_params=pltpu.CompilerParams(
             collective_id=0, has_side_effects=True, vmem_limit_bytes=48 * 1024 * 1024

time: 58.1 us -> 59.4 us (1.022)
  Pallas kernels: 56.7 us -> 58.1 us
    pallas_call x1, Pallas kernels: 56.7 us -> 58.1 us  [on_device(): pl.pallas_call(layer, out_shape=out, in_specs=[hbm_spec] * len(arrays), o...]
where the time goes in v4:
time: 59.4 us; the launch traced here: 59.3 us
  Pallas kernels  58.1 us (98%)
  between operations  0.64 us (1%)
    pallas_call x1, Pallas kernels, on_device(): pl.pallas_call(layer, out_shape=out, in_specs=[hbm_spec] * len(arrays), o...  58.1 us

profile of v4, /device:TPU:1, one launch (start us, length us, event | category | flops | bytes accessed | tf_op | source)
XLA Modules:
  0.0 59.3 jit_solution(11142437561118004402)
XLA Ops:
  0.6 58.1 %shard_map.140 = bf16[8,128]{1,0:T(8,128)(2,1)S(1)} custom-call(bf16[4,128]{1,0:T(4,128)(2,1)} %hidden_any.1, bf16[1,128]{1,0:T(2,128)(2,1)} %bitcast.2, bf16[128,1280]{1,0:T(8,128)(2,1)} %wqkv_any.1, bf16[16,128,128]{2,1,0:T(8,128)(2,1)} %keys_any.1, bf16[16,128,128]{2,1,0:T(8,128)(2,1)} %values_any.1, s32[4,256]{1,0:T(4,128)} %table_any.1, ...), custom_call_target="tpu_custom_call" | custom-call | tf_op jit(solution)/shard_map/pallas_call | solution.py:452
  58.7 0.6 fusion

commit v5 on v3

--- a/solution.py
+++ b/solution.py
@@ -87,7 +87,6 @@
     part_out2,
     part_in2,
     proj_buf,
-    chunk_sum,
     chunk_out,
     chunk_in,
     piece_out,
@@ -128,15 +127,15 @@
         loads[name] = pltpu.make_async_copy(src, dst, load_sem.at[index])
         loads[name].start()
 
+    barrier = pltpu.get_barrier_semaphore()
+
+    @pl.loop(0, PEERS)
+    def announce(i):
+        pl.semaphore_signal(barrier, inc=1, device_id=first_peer(i + 1)[1], device_id_type=MESH)
+
     load(0, "hidden", hidden_any, hidden)
     load(1, "gain", gain_any, gain)
     load(2, "wqkv", wqkv_any, wqkv)
-
-    barrier = pltpu.get_barrier_semaphore()
-
-    @pl.loop(0, PEERS)
-    def announce(i):
-        pl.semaphore_signal(barrier, inc=1, device_id=first_peer(i + 1)[1], device_id_type=MESH)
 
     @pl.loop(0, PEERS)
     def announce_more(i):
@@ -183,12 +182,8 @@
     square = jnp.broadcast_to(jnp.sum(stream * stream, axis=1, keepdims=True), (REQUESTS, LANES))
     loads["wqkv"].wait()
     part = jnp.dot(scaled, wqkv[...], preferred_element_type=f32)
-    part_rows = jnp.concatenate(
-        [part[:, t * LANES : (t + 1) * LANES] for t in range(GROUP + 2)]
-        + [square, jnp.zeros((REQUESTS, LANES), f32)],
-        axis=0,
-    )
-    qkv_out1[...] = part_rows.astype(bf16)
+    total = jnp.concatenate([part, square], axis=1)
+    qkv_out1[...] = total.astype(bf16)
 
     pl.semaphore_wait(barrier, 21)
     exchange(0, first_peer, lambda o: qkv_out1, lambda d: qkv_in1.at[d - 1])
@@ -220,7 +215,6 @@
     sine_part = jnp.where(lane < HEAD_SIZE // 2, -sine_part, sine_part)
 
     arrive(0, qkv_in1)
-    total = part_rows
     for d in range(7):
         total = total + qkv_in1[d].astype(f32)
     qkv_out2[...] = total.astype(bf16)
@@ -240,10 +234,10 @@
     for d in range(7):
         total = total + qkv_in2[d].astype(f32)
 
-    square_all = total[40:44]
-    square_all = jnp.concatenate([square_all, square_all], axis=0)
-    inv_rms = lax.rsqrt(square_all / MODEL_WIDTH + epsilon)
-    joined = total[0:40].reshape(5, 8, LANES) * inv_rms
+    inv_rms = lax.rsqrt(total[:, (GROUP + 2) * LANES :] / MODEL_WIDTH + epsilon)
+    joined = jnp.concatenate(
+        [total[:, t * LANES : (t + 1) * LANES] * inv_rms for t in range(GROUP + 2)], axis=0
+    ).reshape(5, 8, LANES)
     swapped = pltpu.roll(joined.reshape(40, LANES), HEAD_SIZE // 2, 1).reshape(5, 8, LANES)
     turned = joined * cos_part + swapped * sine_part
     queries = turned[0:4].reshape(ROWS, LANES).astype(bf16)
@@ -277,56 +271,59 @@
     mean = (accum / safe).reshape(ROWS, LANES)
     lse = jnp.where(some, peak + jnp.log(safe), neg_fill).reshape(ROWS, 1)
 
-    diagonal = lax.broadcasted_iota(jnp.int32, (ROWS, LANES), 0) == lax.broadcasted_iota(
-        jnp.int32, (ROWS, LANES), 1
-    )
-    lse_row = jnp.sum(jnp.where(diagonal, lse, 0.0), axis=0, keepdims=True)
-    stat_row = lax.broadcasted_iota(jnp.int32, (16, LANES), 0)
-
-    def packed(mean, lse_row):
-        high = lse_row.astype(bf16).astype(f32)
-        rest = lse_row - high
+    tiles = [slice(g * REQUESTS, (g + 1) * REQUESTS) for g in range(GROUP)]
+    means = [mean[rows] for rows in tiles]
+    column = lax.broadcasted_iota(jnp.int32, (REQUESTS, LANES), 1)
+    stats = jnp.zeros((REQUESTS, LANES), f32)
+    for g, rows in enumerate(tiles):
+        stats = jnp.where(column == g, lse[rows], stats)
+
+    def packed(means, stats):
+        high = stats.astype(bf16).astype(f32)
+        rest = stats - high
         middle = rest.astype(bf16).astype(f32)
         low = rest - middle
-        stats = jnp.where(
-            stat_row == 0, high, jnp.where(stat_row == 1, middle, jnp.where(stat_row == 2, low, 0.0))
-        )
-        return jnp.concatenate([mean, stats], axis=0).astype(bf16)
-
-    def merged(mean, lse_row, arrived):
-        means, lses = [mean], [lse_row]
-        for d in range(7):
+        side = high + pltpu.roll(middle, GROUP, 1) + pltpu.roll(low, 2 * GROUP, 1)
+        return jnp.concatenate(means + [side], axis=1).astype(bf16)
+
+    def merged(means, stats, arrived):
+        blocks = [means]
+        lses = [stats]
+        for d in range(PEERS):
             block = arrived[d].astype(f32)
-            means.append(block[0:ROWS])
-            lses.append(block[ROWS : ROWS + 1] + block[ROWS + 1 : ROWS + 2] + block[ROWS + 2 : ROWS + 3])
+            blocks.append([block[:, g * LANES : (g + 1) * LANES] for g in range(GROUP)])
+            side = block[:, GROUP * LANES :]
+            side = side + pltpu.roll(side, LANES - GROUP, 1) + pltpu.roll(side, LANES - 2 * GROUP, 1)
+            lses.append(jnp.where(column < GROUP, side, 0.0))
         best = functools.reduce(jnp.maximum, lses)
         factors = [jnp.exp(part - best) for part in lses]
         whole = functools.reduce(jnp.add, factors)
-        result = None
-        for factor, part in zip(factors, means):
-            column = jnp.sum(jnp.where(diagonal, factor / whole, 0.0), axis=1, keepdims=True)
-            result = column * part if result is None else result + column * part
-        return result, best + jnp.log(whole)
-
-    part_out1[...] = packed(mean, lse_row)
+        factors = [factor / whole for factor in factors]
+        means = [
+            functools.reduce(
+                jnp.add, [factor[:, g : g + 1] * block[g] for factor, block in zip(factors, blocks)]
+            )
+            for g in range(GROUP)
+        ]
+        return means, jnp.where(column < GROUP, best + jnp.log(whole), 0.0)
+
+    part_out1[...] = packed(means, stats)
     exchange(2, first_peer, lambda o: part_out1, lambda d: part_in1.at[d - 1])
     loads["wout"].wait()
     loads["fgain"].wait()
     departed(1, qkv_in2)
     arrive(2, part_in1)
-    mean, lse_row = merged(mean, lse_row, part_in1)
-    part_out2[...] = packed(mean, lse_row)
+    means, stats = merged(means, stats, part_in1)
+    part_out2[...] = packed(means, stats)
     exchange(3, second_peer, lambda o: part_out2, lambda d: part_in2.at[d - 1])
     loads["wgate"].wait()
     loads["wup"].wait()
     loads["wdown"].wait()
     departed(2, part_in1)
     arrive(3, part_in2)
-    mean, _ = merged(mean, lse_row, part_in2)
-
-    attention = jnp.concatenate(
-        [mean[g * REQUESTS : (g + 1) * REQUESTS] for g in range(GROUP)], axis=1
-    ).astype(bf16)
+    means, _ = merged(means, stats, part_in2)
+
+    attention = jnp.concatenate(means, axis=1).astype(bf16)
     proj_buf[head] = jnp.dot(attention, wout[...], preferred_element_type=f32)
     exchange(4, head_peer, lambda o: proj_buf.at[head], lambda d: proj_buf.at[head])
     departed(3, part_in2)
@@ -339,21 +336,23 @@
     ffn = (after * fgain[...].astype(f32)).astype(bf16)
     square = jnp.broadcast_to(jnp.sum(after * after, axis=1, keepdims=True), (REQUESTS, LANES))
 
-    def chunk_of(owner):
-        span = pl.ds(pl.multiple_of(owner * CHUNK, CHUNK), CHUNK)
-        gate_part = jnp.dot(ffn, wgate[:, span], preferred_element_type=f32)
-        up_part = jnp.dot(ffn, wup[:, span], preferred_element_type=f32)
-        return jnp.concatenate([gate_part, up_part, square], axis=1)
+    gate_part = jnp.dot(ffn, wgate[...], preferred_element_type=f32)
+    up_part = jnp.dot(ffn, wup[...], preferred_element_type=f32)
+    for c in range(OWNERS):
+        span = slice(c * CHUNK, (c + 1) * CHUNK)
+        chunk_out[c] = jnp.concatenate([gate_part[:, span], up_part[:, span], square], axis=1).astype(bf16)
 
     owns = first < OWNERS
-    for d in RING_ORDER:
+
+    @pl.loop(0, PEERS)
+    def send_chunk(i):
+        d = ring_distance(i)
         other, device = first_peer(d)
-        chunk_out[d - 1] = chunk_of(jnp.minimum(other, OWNERS - 1)).astype(bf16)
 
         @pl.when(other < OWNERS)
-        def send_chunk():
+        def start():
             pltpu.make_async_remote_copy(
-                src_ref=chunk_out.at[d - 1],
+                src_ref=chunk_out.at[other],
                 dst_ref=chunk_in.at[d - 1],
                 send_sem=send_sem.at[5],
                 recv_sem=recv_sem.at[5],
@@ -361,7 +360,6 @@
                 device_id_type=MESH,
             ).start()
 
-    chunk_sum[...] = chunk_of(jnp.minimum(first, OWNERS - 1))
     down_sum[...] = jnp.zeros((REQUESTS, LANES), f32)
     departed(4, proj_buf)
 
@@ -371,7 +369,7 @@
 
     @pl.when(owns)
     def own_chunk():
-        total = chunk_sum[...]
+        total = chunk_out[first].astype(f32)
         arrive(5, chunk_in)
         for d in range(PEERS):
             total = total + chunk_in[d].astype(f32)
@@ -463,7 +461,7 @@
     hbm_spec = pl.BlockSpec(memory_space=pltpu.HBM)
     vmem_spec = pl.BlockSpec(memory_space=pltpu.VMEM)
     out = pltpu.VMEM((2 * requests, width), bf16)
-    rows = 48
+    qkv_width, part_width = (GROUP + 3) * LANES, (GROUP + 1) * LANES
     both = pl.pallas_call(
         layer,
         out_shape=out,
@@ -474,19 +472,18 @@
         ]
         + [
             pltpu.SemaphoreType.DMA((len(arrays),)),
-            pltpu.VMEM((rows, LANES), bf16),
-            pltpu.VMEM((7, rows, LANES), bf16),
-            pltpu.VMEM((rows, LANES), bf16),
-            pltpu.VMEM((7, rows, LANES), bf16),
+            pltpu.VMEM((requests, qkv_width), bf16),
+            pltpu.VMEM((PEERS, requests, qkv_width), bf16),
+            pltpu.VMEM((requests, qkv_width), bf16),
+            pltpu.VMEM((PEERS, requests, qkv_width), bf16),
             pltpu.VMEM((8, SLOTS * PAGE_TOKENS), f32),
             pltpu.VMEM((HEAD_SIZE, SLOTS * PAGE_TOKENS), bf16),
-            pltpu.VMEM((rows, LANES), bf16),
-            pltpu.VMEM((7, rows, LANES), bf16),
-            pltpu.VMEM((rows, LANES), bf16),
-            pltpu.VMEM((7, rows, LANES), bf16),
+            pltpu.VMEM((requests, part_width), bf16),
+            pltpu.VMEM((PEERS, requests, part_width), bf16),
+            pltpu.VMEM((requests, part_width), bf16),
+            pltpu.VMEM((PEERS, requests, part_width), bf16),
             pltpu.VMEM((HEADS, REQUESTS, LANES), f32),
-            pltpu.VMEM((REQUESTS, 2 * CHUNK + LANES), f32),
-            pltpu.VMEM((PEERS, REQUESTS, 2 * CHUNK + LANES), bf16),
+            pltpu.VMEM((SIDE, REQUESTS, 2 * CHUNK + LANES), bf16),
             pltpu.VMEM((PEERS, REQUESTS, 2 * CHUNK + LANES), bf16),
             pltpu.VMEM((REQUESTS, 2 * CHUNK + LANES), bf16),
             pltpu.VMEM((PEERS, REQUESTS, 2 * CHUNK + LANES), bf16),

time: 58.1 us -> 58.3 us (level)
  no operation moved by 1% of the time
where the time goes in v5:
time: 58.3 us; the launch traced here: 58.2 us
  Pallas kernels  57 us (98%)
  between operations  0.64 us (1%)
    pallas_call x1, Pallas kernels, on_device(): pl.pallas_call(layer, out_shape=out, in_specs=[hbm_spec] * len(arrays), o...  57 us

profile of v5, /device:TPU:1, one launch (start us, length us, event | category | flops | bytes accessed | tf_op | source)
XLA Modules:
  0.0 58.2 jit_solution(3239877886040698687)
XLA Ops:
  0.6 57.0 %shard_map.140 = bf16[8,128]{1,0:T(8,128)(2,1)S(1)} custom-call(bf16[4,128]{1,0:T(4,128)(2,1)} %hidden_any.1, bf16[1,128]{1,0:T(2,128)(2,1)} %bitcast.2, bf16[128,1280]{1,0:T(8,128)(2,1)} %wqkv_any.1, bf16[16,128,128]{2,1,0:T(8,128)(2,1)} %keys_any.1, bf16[16,128,128]{2,1,0:T(8,128)(2,1)} %values_any.1, s32[4,256]{1,0:T(4,128)} %table_any.1, ...), custom_call_target="tpu_custom_call" | custom-call | tf_op jit(solution)/shard_map/pallas_call | solution.py:465
  57.6 0.6 fusion

commit v6 on v5

--- a/solution.py
+++ b/solution.py
@@ -29,9 +29,8 @@
 bf16 = jnp.bfloat16
 
 PEERS = 7
-RING_ORDER = (4, 3, 5, 2, 6, 1, 7)
-OWNERS = 7
-CHUNK = 512
+CLASSES = 4
+CHUNK = 896
 
 
 def ring_distance(i):
@@ -92,11 +91,9 @@
     piece_out,
     piece_in,
     act_buf,
-    down_sum,
     down_buf,
     send_sem,
     recv_sem,
-    act_sem,
 ):
     seq = lax.axis_index("seq")
     head = lax.axis_index("head")
@@ -131,27 +128,19 @@
 
     @pl.loop(0, PEERS)
     def announce(i):
-        pl.semaphore_signal(barrier, inc=1, device_id=first_peer(i + 1)[1], device_id_type=MESH)
+        pl.semaphore_signal(barrier, inc=1, device_id=first_peer(ring_distance(i))[1], device_id_type=MESH)
 
     load(0, "hidden", hidden_any, hidden)
     load(1, "gain", gain_any, gain)
     load(2, "wqkv", wqkv_any, wqkv)
+    load(3, "table", table_any, table)
+    load(4, "lengths", len_any, len_ref)
+    load(5, "freq", freq_any, freq_ref)
 
     @pl.loop(0, PEERS)
     def announce_more(i):
         for peer in (second_peer, head_peer):
-            pl.semaphore_signal(barrier, inc=1, device_id=peer(i + 1)[1], device_id_type=MESH)
-
-    load(3, "table", table_any, table)
-    load(4, "lengths", len_any, len_ref)
-    load(5, "freq", freq_any, freq_ref)
-    load(6, "keys", keys_any, keys)
-    load(7, "values", values_any, values)
-    load(8, "wout", wout_any, wout)
-    load(9, "fgain", fgain_any, fgain)
-    load(10, "wgate", wgate_any, wgate)
-    load(11, "wup", wup_any, wup)
-    load(12, "wdown", wdown_any, wdown)
+            pl.semaphore_signal(barrier, inc=1, device_id=peer(ring_distance(i))[1], device_id_type=MESH)
 
     def exchange(step, peer, src_of, dst_of):
         @pl.loop(0, PEERS)
@@ -167,8 +156,8 @@
                 device_id_type=MESH,
             ).start()
 
-    def arrive(step, blocks):
-        some = blocks.at[pl.ds(0, PEERS)]
+    def arrive(step, blocks, count=PEERS):
+        some = blocks.at[pl.ds(0, count)]
         pltpu.make_async_copy(some, some, recv_sem.at[step]).wait()
 
     def departed(step, blocks, count=PEERS):
@@ -187,6 +176,14 @@
 
     pl.semaphore_wait(barrier, 21)
     exchange(0, first_peer, lambda o: qkv_out1, lambda d: qkv_in1.at[d - 1])
+
+    load(6, "keys", keys_any, keys)
+    load(7, "values", values_any, values)
+    load(8, "wout", wout_any, wout)
+    load(9, "fgain", fgain_any, fgain)
+    load(10, "wgate", wgate_any, wgate)
+    load(11, "wup", wup_any, wup)
+    load(12, "wdown", wdown_any, wdown)
 
     sub = lax.broadcasted_iota(jnp.int32, (8, 1), 0)
     request = lax.rem(sub, REQUESTS)
@@ -338,88 +335,46 @@
 
     gate_part = jnp.dot(ffn, wgate[...], preferred_element_type=f32)
     up_part = jnp.dot(ffn, wup[...], preferred_element_type=f32)
-    for c in range(OWNERS):
+    for c in range(CLASSES):
         span = slice(c * CHUNK, (c + 1) * CHUNK)
         chunk_out[c] = jnp.concatenate([gate_part[:, span], up_part[:, span], square], axis=1).astype(bf16)
 
-    owns = first < OWNERS
-
-    @pl.loop(0, PEERS)
-    def send_chunk(i):
-        d = ring_distance(i)
-        other, device = first_peer(d)
-
-        @pl.when(other < OWNERS)
-        def start():
-            pltpu.make_async_remote_copy(
-                src_ref=chunk_out.at[other],
-                dst_ref=chunk_in.at[d - 1],
-                send_sem=send_sem.at[5],
-                recv_sem=recv_sem.at[5],
-                device_id=device,
-                device_id_type=MESH,
-            ).start()
-
-    down_sum[...] = jnp.zeros((REQUESTS, LANES), f32)
+    exchange(
+        5, first_peer, lambda o: chunk_out.at[lax.rem(o, CLASSES)], lambda d: chunk_in.at[d - 1]
+    )
+    mine = lax.rem(first, CLASSES)
+    total = chunk_out[mine].astype(f32)
     departed(4, proj_buf)
-
-    def down_of(owner):
-        span = pl.ds(pl.multiple_of(owner * CHUNK, CHUNK), CHUNK)
-        down_sum[...] += jnp.dot(act_buf[owner], wdown[span, :], preferred_element_type=f32)
-
-    @pl.when(owns)
-    def own_chunk():
-        total = chunk_out[first].astype(f32)
-        arrive(5, chunk_in)
-        for d in range(PEERS):
-            total = total + chunk_in[d].astype(f32)
-        piece_out[...] = total.astype(bf16)
-        exchange(6, second_peer, lambda o: piece_out, lambda d: piece_in.at[d - 1])
-        departed(5, chunk_in, OWNERS - 1)
-        arrive(6, piece_in)
-        for d in range(PEERS):
-            total = total + piece_in[d].astype(f32)
-        inv_norm = lax.rsqrt(total[:, 2 * CHUNK : 2 * CHUNK + 1] / MODEL_WIDTH + epsilon)
-        gate = total[:, :CHUNK] * inv_norm
-        act = gate / (1.0 + jnp.exp(-gate)) * (total[:, CHUNK : 2 * CHUNK] * inv_norm)
-        act_buf[first] = act.astype(bf16)
-
-        @pl.loop(0, PEERS)
-        def send_act(i):
-            d = ring_distance(i)
-            other, device = first_peer(d)
-            pltpu.make_async_remote_copy(
-                src_ref=act_buf.at[first],
-                dst_ref=act_buf.at[first],
-                send_sem=send_sem.at[7],
-                recv_sem=act_sem.at[d - 1],
-                device_id=device,
-                device_id_type=MESH,
-            ).start()
-
-        departed(6, piece_in)
-        down_of(first)
-
-    @pl.when(jnp.logical_not(owns))
-    def no_chunk():
-        departed(5, chunk_in, OWNERS)
-
-    for d in reversed(RING_ORDER):
-        owner = lax.rem(first + SIDE - d, SIDE)
-
-        @pl.when(owner < OWNERS)
-        def take_act():
-            block = act_buf.at[owner]
-            pltpu.make_async_copy(block, block, act_sem.at[d - 1]).wait()
-            down_of(owner)
-
-    down_buf[head] = down_sum[...]
+    arrive(5, chunk_in)
+    for d in range(PEERS):
+        total = total + chunk_in[d].astype(f32)
+    piece_out[...] = total.astype(bf16)
+    exchange(6, second_peer, lambda o: piece_out, lambda d: piece_in.at[d - 1])
+    departed(5, chunk_in)
+    arrive(6, piece_in)
+    for d in range(PEERS):
+        total = total + piece_in[d].astype(f32)
+    inv_norm = lax.rsqrt(total[:, 2 * CHUNK : 2 * CHUNK + 1] / MODEL_WIDTH + epsilon)
+    gate = total[:, :CHUNK] * inv_norm
+    act = gate / (1.0 + jnp.exp(-gate)) * (total[:, CHUNK : 2 * CHUNK] * inv_norm)
+    act_buf[mine] = act.astype(bf16)
+
+    for d in (2, 1, SIDE - 1):
+        _, device = first_peer(d)
+        pltpu.make_async_remote_copy(
+            src_ref=act_buf.at[mine],
+            dst_ref=act_buf.at[mine],
+            send_sem=send_sem.at[7],
+            recv_sem=recv_sem.at[7],
+            device_id=device,
+            device_id_type=MESH,
+        ).start()
+    departed(6, piece_in)
+    arrive(7, act_buf, CLASSES - 1)
+    units = jnp.concatenate([act_buf[c] for c in range(CLASSES)], axis=1)
+    down_buf[head] = jnp.dot(units, wdown[...], preferred_element_type=f32)
     exchange(8, head_peer, lambda o: down_buf.at[head], lambda d: down_buf.at[head])
-
-    @pl.when(owns)
-    def act_sent():
-        departed(7, act_buf)
-
+    departed(7, act_buf, CLASSES - 1)
     arrive(8, down_buf)
     down = down_buf[0]
     for h in range(1, HEADS):
@@ -483,16 +438,14 @@
             pltpu.VMEM((requests, part_width), bf16),
             pltpu.VMEM((PEERS, requests, part_width), bf16),
             pltpu.VMEM((HEADS, REQUESTS, LANES), f32),
-            pltpu.VMEM((SIDE, REQUESTS, 2 * CHUNK + LANES), bf16),
+            pltpu.VMEM((CLASSES, REQUESTS, 2 * CHUNK + LANES), bf16),
             pltpu.VMEM((PEERS, REQUESTS, 2 * CHUNK + LANES), bf16),
             pltpu.VMEM((REQUESTS, 2 * CHUNK + LANES), bf16),
             pltpu.VMEM((PEERS, REQUESTS, 2 * CHUNK + LANES), bf16),
-            pltpu.VMEM((SIDE, REQUESTS, CHUNK), bf16),
-            pltpu.VMEM((REQUESTS, LANES), f32),
+            pltpu.VMEM((CLASSES, REQUESTS, CHUNK), bf16),
             pltpu.VMEM((HEADS, REQUESTS, LANES), f32),
             pltpu.SemaphoreType.DMA((9,)),
             pltpu.SemaphoreType.DMA((9,)),
-            pltpu.SemaphoreType.DMA((PEERS,)),
         ],
         compiler_params=pltpu.CompilerParams(
             collective_id=0, has_side_effects=True, vmem_limit_bytes=48 * 1024 * 1024

time: 58.3 us -> 57.6 us (0.988)
  Pallas kernels: 57 us -> 56.3 us
    pallas_call x1, Pallas kernels: 57 us -> 56.3 us  [on_device(): pl.pallas_call(layer, out_shape=out, in_specs=[hbm_spec] * len(arrays), o...]
where the time goes in v6:
time: 57.6 us; the launch traced here: 57.5 us
  Pallas kernels  56.3 us (98%)
  between operations  0.64 us (1%)
    pallas_call x1, Pallas kernels, on_device(): pl.pallas_call(layer, out_shape=out, in_specs=[hbm_spec] * len(arrays), o...  56.3 us

profile of v6, /device:TPU:1, one launch (start us, length us, event | category | flops | bytes accessed | tf_op | source)
XLA Modules:
  0.0 57.5 jit_solution(650290366209351991)
XLA Ops:
  0.6 56.3 %shard_map.140 = bf16[8,128]{1,0:T(8,128)(2,1)S(1)} custom-call(bf16[4,128]{1,0:T(4,128)(2,1)} %hidden_any.1, bf16[1,128]{1,0:T(2,128)(2,1)} %bitcast.2, bf16[128,1280]{1,0:T(8,128)(2,1)} %wqkv_any.1, bf16[16,128,128]{2,1,0:T(8,128)(2,1)} %keys_any.1, bf16[16,128,128]{2,1,0:T(8,128)(2,1)} %values_any.1, s32[4,256]{1,0:T(4,128)} %table_any.1, ...), custom_call_target="tpu_custom_call" | custom-call | tf_op jit(solution)/shard_map/pallas_call | solution.py:420
  56.9 0.6 fusion

commit v7 on v6

--- a/solution.py
+++ b/solution.py
@@ -86,6 +86,7 @@
     part_out2,
     part_in2,
     proj_buf,
+    chunk_sum,
     chunk_out,
     chunk_in,
     piece_out,
@@ -94,6 +95,7 @@
     down_buf,
     send_sem,
     recv_sem,
+    act_sem,
 ):
     seq = lax.axis_index("seq")
     head = lax.axis_index("head")
@@ -333,17 +335,28 @@
     ffn = (after * fgain[...].astype(f32)).astype(bf16)
     square = jnp.broadcast_to(jnp.sum(after * after, axis=1, keepdims=True), (REQUESTS, LANES))
 
-    gate_part = jnp.dot(ffn, wgate[...], preferred_element_type=f32)
-    up_part = jnp.dot(ffn, wup[...], preferred_element_type=f32)
-    for c in range(CLASSES):
-        span = slice(c * CHUNK, (c + 1) * CHUNK)
-        chunk_out[c] = jnp.concatenate([gate_part[:, span], up_part[:, span], square], axis=1).astype(bf16)
-
-    exchange(
-        5, first_peer, lambda o: chunk_out.at[lax.rem(o, CLASSES)], lambda d: chunk_in.at[d - 1]
-    )
+
+    for away, distances in ((0, (4,)), (3, (3, 7)), (1, (5, 1)), (2, (6, 2))):
+        wanted = lax.rem(first + away, CLASSES)
+        span = pl.ds(pl.multiple_of(wanted * CHUNK, LANES), CHUNK)
+        gate_part = jnp.dot(ffn, wgate[:, span], preferred_element_type=f32)
+        up_part = jnp.dot(ffn, wup[:, span], preferred_element_type=f32)
+        chunk = jnp.concatenate([gate_part, up_part, square], axis=1)
+        chunk_out[away] = chunk.astype(bf16)
+        if away == 0:
+            chunk_sum[...] = chunk
+        for d in distances:
+            _, device = first_peer(d)
+            pltpu.make_async_remote_copy(
+                src_ref=chunk_out.at[away],
+                dst_ref=chunk_in.at[d - 1],
+                send_sem=send_sem.at[5],
+                recv_sem=recv_sem.at[5],
+                device_id=device,
+                device_id_type=MESH,
+            ).start()
     mine = lax.rem(first, CLASSES)
-    total = chunk_out[mine].astype(f32)
+    total = chunk_sum[...]
     departed(4, proj_buf)
     arrive(5, chunk_in)
     for d in range(PEERS):
@@ -359,20 +372,29 @@
     act = gate / (1.0 + jnp.exp(-gate)) * (total[:, CHUNK : 2 * CHUNK] * inv_norm)
     act_buf[mine] = act.astype(bf16)
 
-    for d in (2, 1, SIDE - 1):
+    for k, d in enumerate((2, 1, SIDE - 1)):
         _, device = first_peer(d)
         pltpu.make_async_remote_copy(
             src_ref=act_buf.at[mine],
             dst_ref=act_buf.at[mine],
             send_sem=send_sem.at[7],
-            recv_sem=recv_sem.at[7],
+            recv_sem=act_sem.at[k],
             device_id=device,
             device_id_type=MESH,
         ).start()
+
+    def down_of(owned):
+        span = pl.ds(pl.multiple_of(owned * CHUNK, LANES), CHUNK)
+        return jnp.dot(act_buf[owned], wdown[span, :], preferred_element_type=f32)
+
+    part = down_of(mine)
     departed(6, piece_in)
-    arrive(7, act_buf, CLASSES - 1)
-    units = jnp.concatenate([act_buf[c] for c in range(CLASSES)], axis=1)
-    down_buf[head] = jnp.dot(units, wdown[...], preferred_element_type=f32)
+    for k, d in ((1, 1), (2, SIDE - 1), (0, 2)):
+        owned = lax.rem(first + SIDE - d, CLASSES)
+        block = act_buf.at[owned]
+        pltpu.make_async_copy(block, block, act_sem.at[k]).wait()
+        part = part + down_of(owned)
+    down_buf[head] = part
     exchange(8, head_peer, lambda o: down_buf.at[head], lambda d: down_buf.at[head])
     departed(7, act_buf, CLASSES - 1)
     arrive(8, down_buf)
@@ -438,6 +460,7 @@
             pltpu.VMEM((requests, part_width), bf16),
             pltpu.VMEM((PEERS, requests, part_width), bf16),
             pltpu.VMEM((HEADS, REQUESTS, LANES), f32),
+            pltpu.VMEM((REQUESTS, 2 * CHUNK + LANES), f32),
             pltpu.VMEM((CLASSES, REQUESTS, 2 * CHUNK + LANES), bf16),
             pltpu.VMEM((PEERS, REQUESTS, 2 * CHUNK + LANES), bf16),
             pltpu.VMEM((REQUESTS, 2 * CHUNK + LANES), bf16),
@@ -446,6 +469,7 @@
             pltpu.VMEM((HEADS, REQUESTS, LANES), f32),
             pltpu.SemaphoreType.DMA((9,)),
             pltpu.SemaphoreType.DMA((9,)),
+            pltpu.SemaphoreType.DMA((CLASSES - 1,)),
         ],
         compiler_params=pltpu.CompilerParams(
             collective_id=0, has_side_effects=True, vmem_limit_bytes=48 * 1024 * 1024

time: 57.6 us -> 57.9 us (level)
  no operation moved by 1% of the time
where the time goes in v7:
time: 57.9 us; the launch traced here: 57.8 us
  Pallas kernels  56.6 us (98%)
  between operations  0.64 us (1%)
    pallas_call x1, Pallas kernels, on_device(): pl.pallas_call(layer, out_shape=out, in_specs=[hbm_spec] * len(arrays), o...  56.6 us

profile of v7, /device:TPU:1, one launch (start us, length us, event | category | flops | bytes accessed | tf_op | source)
XLA Modules:
  0.0 57.8 jit_solution(1445005292233953157)
XLA Ops:
  0.6 56.6 %shard_map.140 = bf16[8,128]{1,0:T(8,128)(2,1)S(1)} custom-call(bf16[4,128]{1,0:T(4,128)(2,1)} %hidden_any.1, bf16[1,128]{1,0:T(2,128)(2,1)} %bitcast.2, bf16[128,1280]{1,0:T(8,128)(2,1)} %wqkv_any.1, bf16[16,128,128]{2,1,0:T(8,128)(2,1)} %keys_any.1, bf16[16,128,128]{2,1,0:T(8,128)(2,1)} %values_any.1, s32[4,256]{1,0:T(4,128)} %table_any.1, ...), custom_call_target="tpu_custom_call" | custom-call | tf_op jit(solution)/shard_map/pallas_call | solution.py:442
  57.2 0.6 fusion

commit v8 on v7

--- a/solution.py
+++ b/solution.py
@@ -32,9 +32,7 @@
 CLASSES = 4
 CHUNK = 896
 
-
-def ring_distance(i):
-    return 4 + ((i + 1) // 2) * (1 - 2 * lax.rem(i, 2))
+RING_ORDER = (4, 3, 5, 2, 6, 1, 7)
 
 
 def rope_frequencies():
@@ -126,11 +124,14 @@
         loads[name] = pltpu.make_async_copy(src, dst, load_sem.at[index])
         loads[name].start()
 
+    first_peers = {d: first_peer(d) for d in RING_ORDER}
+    second_peers = {d: second_peer(d) for d in RING_ORDER}
+    head_peers = {d: head_peer(d) for d in RING_ORDER}
+
     barrier = pltpu.get_barrier_semaphore()
 
-    @pl.loop(0, PEERS)
-    def announce(i):
-        pl.semaphore_signal(barrier, inc=1, device_id=first_peer(ring_distance(i))[1], device_id_type=MESH)
+    for d in RING_ORDER:
+        pl.semaphore_signal(barrier, inc=1, device_id=first_peers[d][1], device_id_type=MESH)
 
     load(0, "hidden", hidden_any, hidden)
     load(1, "gain", gain_any, gain)
@@ -139,16 +140,13 @@
     load(4, "lengths", len_any, len_ref)
     load(5, "freq", freq_any, freq_ref)
 
-    @pl.loop(0, PEERS)
-    def announce_more(i):
-        for peer in (second_peer, head_peer):
-            pl.semaphore_signal(barrier, inc=1, device_id=peer(ring_distance(i))[1], device_id_type=MESH)
-
-    def exchange(step, peer, src_of, dst_of):
-        @pl.loop(0, PEERS)
-        def send(i):
-            d = ring_distance(i)
-            other, device = peer(d)
+    for d in RING_ORDER:
+        for peers in (second_peers, head_peers):
+            pl.semaphore_signal(barrier, inc=1, device_id=peers[d][1], device_id_type=MESH)
+
+    def exchange(step, peers, src_of, dst_of):
+        for d in RING_ORDER:
+            other, device = peers[d]
             pltpu.make_async_remote_copy(
                 src_ref=src_of(other),
                 dst_ref=dst_of(d),
@@ -177,7 +175,7 @@
     qkv_out1[...] = total.astype(bf16)
 
     pl.semaphore_wait(barrier, 21)
-    exchange(0, first_peer, lambda o: qkv_out1, lambda d: qkv_in1.at[d - 1])
+    exchange(0, first_peers, lambda o: qkv_out1, lambda d: qkv_in1.at[d - 1])
 
     load(6, "keys", keys_any, keys)
     load(7, "values", values_any, values)
@@ -217,7 +215,7 @@
     for d in range(7):
         total = total + qkv_in1[d].astype(f32)
     qkv_out2[...] = total.astype(bf16)
-    exchange(1, second_peer, lambda o: qkv_out2, lambda d: qkv_in2.at[d - 1])
+    exchange(1, second_peers, lambda o: qkv_out2, lambda d: qkv_in2.at[d - 1])
     loads["keys"].wait()
 
     @pl.loop(0, SLOTS // 4)
@@ -228,7 +226,6 @@
             keys_turned[:, span] = keys[j].T
 
     loads["values"].wait()
-    departed(0, qkv_in1)
     arrive(1, qkv_in2)
     for d in range(7):
         total = total + qkv_in2[d].astype(f32)
@@ -307,25 +304,22 @@
         return means, jnp.where(column < GROUP, best + jnp.log(whole), 0.0)
 
     part_out1[...] = packed(means, stats)
-    exchange(2, first_peer, lambda o: part_out1, lambda d: part_in1.at[d - 1])
+    exchange(2, first_peers, lambda o: part_out1, lambda d: part_in1.at[d - 1])
     loads["wout"].wait()
     loads["fgain"].wait()
-    departed(1, qkv_in2)
     arrive(2, part_in1)
     means, stats = merged(means, stats, part_in1)
     part_out2[...] = packed(means, stats)
-    exchange(3, second_peer, lambda o: part_out2, lambda d: part_in2.at[d - 1])
+    exchange(3, second_peers, lambda o: part_out2, lambda d: part_in2.at[d - 1])
     loads["wgate"].wait()
     loads["wup"].wait()
     loads["wdown"].wait()
-    departed(2, part_in1)
     arrive(3, part_in2)
     means, _ = merged(means, stats, part_in2)
 
     attention = jnp.concatenate(means, axis=1).astype(bf16)
     proj_buf[head] = jnp.dot(attention, wout[...], preferred_element_type=f32)
-    exchange(4, head_peer, lambda o: proj_buf.at[head], lambda d: proj_buf.at[head])
-    departed(3, part_in2)
+    exchange(4, head_peers, lambda o: proj_buf.at[head], lambda d: proj_buf.at[head])
     arrive(4, proj_buf)
     projected = proj_buf[0]
     for h in range(1, HEADS):
@@ -346,7 +340,7 @@
         if away == 0:
             chunk_sum[...] = chunk
         for d in distances:
-            _, device = first_peer(d)
+            _, device = first_peers[d]
             pltpu.make_async_remote_copy(
                 src_ref=chunk_out.at[away],
                 dst_ref=chunk_in.at[d - 1],
@@ -357,13 +351,11 @@
             ).start()
     mine = lax.rem(first, CLASSES)
     total = chunk_sum[...]
-    departed(4, proj_buf)
     arrive(5, chunk_in)
     for d in range(PEERS):
         total = total + chunk_in[d].astype(f32)
     piece_out[...] = total.astype(bf16)
-    exchange(6, second_peer, lambda o: piece_out, lambda d: piece_in.at[d - 1])
-    departed(5, chunk_in)
+    exchange(6, second_peers, lambda o: piece_out, lambda d: piece_in.at[d - 1])
     arrive(6, piece_in)
     for d in range(PEERS):
         total = total + piece_in[d].astype(f32)
@@ -373,7 +365,7 @@
     act_buf[mine] = act.astype(bf16)
 
     for k, d in enumerate((2, 1, SIDE - 1)):
-        _, device = first_peer(d)
+        _, device = first_peers[d]
         pltpu.make_async_remote_copy(
             src_ref=act_buf.at[mine],
             dst_ref=act_buf.at[mine],
@@ -388,20 +380,26 @@
         return jnp.dot(act_buf[owned], wdown[span, :], preferred_element_type=f32)
 
     part = down_of(mine)
-    departed(6, piece_in)
     for k, d in ((1, 1), (2, SIDE - 1), (0, 2)):
         owned = lax.rem(first + SIDE - d, CLASSES)
         block = act_buf.at[owned]
         pltpu.make_async_copy(block, block, act_sem.at[k]).wait()
         part = part + down_of(owned)
     down_buf[head] = part
-    exchange(8, head_peer, lambda o: down_buf.at[head], lambda d: down_buf.at[head])
-    departed(7, act_buf, CLASSES - 1)
+    exchange(8, head_peers, lambda o: down_buf.at[head], lambda d: down_buf.at[head])
     arrive(8, down_buf)
     down = down_buf[0]
     for h in range(1, HEADS):
         down = down + down_buf[h]
     both_ref[...] = jnp.concatenate([after, after + down], axis=0).astype(bf16)
+    departed(0, qkv_in1)
+    departed(1, qkv_in2)
+    departed(2, part_in1)
+    departed(3, part_in2)
+    departed(4, proj_buf)
+    departed(5, chunk_in)
+    departed(6, piece_in)
+    departed(7, act_buf, CLASSES - 1)
     departed(8, down_buf)
 
 

time: 57.9 us -> 58.3 us (level)
  no operation moved by 1% of the time
where the time goes in v8:
time: 58.3 us; the launch traced here: 58.2 us
  Pallas kernels  57 us (98%)
  between operations  0.64 us (1%)
    pallas_call x1, Pallas kernels, on_device(): pl.pallas_call(layer, out_shape=out, in_specs=[hbm_spec] * len(arrays), o...  57 us

profile of v8, /device:TPU:1, one launch (start us, length us, event | category | flops | bytes accessed | tf_op | source)
XLA Modules:
  0.0 58.2 jit_solution(1223795964280114005)
XLA Ops:
  0.6 57.0 %shard_map.140 = bf16[8,128]{1,0:T(8,128)(2,1)S(1)} custom-call(bf16[4,128]{1,0:T(4,128)(2,1)} %hidden_any.1, bf16[1,128]{1,0:T(2,128)(2,1)} %bitcast.2, bf16[128,1280]{1,0:T(8,128)(2,1)} %wqkv_any.1, bf16[16,128,128]{2,1,0:T(8,128)(2,1)} %keys_any.1, bf16[16,128,128]{2,1,0:T(8,128)(2,1)} %values_any.1, s32[4,256]{1,0:T(4,128)} %table_any.1, ...), custom_call_target="tpu_custom_call" | custom-call | tf_op jit(solution)/shard_map/pallas_call | solution.py:440
  57.6 0.6 fusion

commit v9 on v6

--- a/solution.py
+++ b/solution.py
@@ -29,8 +29,22 @@
 bf16 = jnp.bfloat16
 
 PEERS = 7
-CLASSES = 4
-CHUNK = 896
+OWNERS = 14
+CHUNK = 256
+DEVICES = 64
+
+
+def near_half():
+    chosen = []
+    for dy in range(SIDE):
+        for dz in range(SIDE):
+            hops = min(dy, SIDE - dy) + min(dz, SIDE - dz)
+            if hops < 4 or (hops == 4 and dy < 4):
+                chosen.append((-hops, dy, dz))
+    return [(dy, dz) for hops, dy, dz in sorted(chosen) if hops]
+
+
+NEAR = near_half()
 
 
 def ring_distance(i):
@@ -86,10 +100,9 @@
     part_out2,
     part_in2,
     proj_buf,
+    chunk_sum,
     chunk_out,
     chunk_in,
-    piece_out,
-    piece_in,
     act_buf,
     down_buf,
     send_sem,
@@ -335,52 +348,84 @@
 
     gate_part = jnp.dot(ffn, wgate[...], preferred_element_type=f32)
     up_part = jnp.dot(ffn, wup[...], preferred_element_type=f32)
-    for c in range(CLASSES):
-        span = slice(c * CHUNK, (c + 1) * CHUNK)
-        chunk_out[c] = jnp.concatenate([gate_part[:, span], up_part[:, span], square], axis=1).astype(bf16)
-
-    exchange(
-        5, first_peer, lambda o: chunk_out.at[lax.rem(o, CLASSES)], lambda d: chunk_in.at[d - 1]
-    )
-    mine = lax.rem(first, CLASSES)
-    total = chunk_out[mine].astype(f32)
+    for p in range(OWNERS):
+        span = slice(p * CHUNK, (p + 1) * CHUNK)
+        chunk_out[p] = jnp.concatenate([gate_part[:, span], up_part[:, span], square], axis=1).astype(bf16)
+
+    place = lax.rem(row_y, 4) * SIDE + lax.rem(row_z + 4 * (row_y // 4), SIDE)
+    mine_p = place // 2
+    owns = (lax.rem(place, 2) == core) & (mine_p < OWNERS)
+
+    @pl.loop(0, 2 * OWNERS)
+    def send_chunk(i):
+        again = lax.rem(i, 2)
+        p = lax.rem(mine_p + OWNERS // 2 + i // 2, OWNERS)
+        spot = 2 * p + core
+        owner = (spot // SIDE + 4 * again) * SIDE + lax.rem(spot + 4 * again, SIDE)
+
+        @pl.when(owner != seq)
+        def start():
+            pltpu.make_async_remote_copy(
+                src_ref=chunk_out.at[p],
+                dst_ref=chunk_in.at[seq],
+                send_sem=send_sem.at[5],
+                recv_sem=recv_sem.at[5],
+                device_id=(owner, head),
+                device_id_type=MESH,
+            ).start()
+
     departed(4, proj_buf)
-    arrive(5, chunk_in)
-    for d in range(PEERS):
-        total = total + chunk_in[d].astype(f32)
-    piece_out[...] = total.astype(bf16)
-    exchange(6, second_peer, lambda o: piece_out, lambda d: piece_in.at[d - 1])
-    departed(5, chunk_in)
-    arrive(6, piece_in)
-    for d in range(PEERS):
-        total = total + piece_in[d].astype(f32)
-    inv_norm = lax.rsqrt(total[:, 2 * CHUNK : 2 * CHUNK + 1] / MODEL_WIDTH + epsilon)
-    gate = total[:, :CHUNK] * inv_norm
-    act = gate / (1.0 + jnp.exp(-gate)) * (total[:, CHUNK : 2 * CHUNK] * inv_norm)
-    act_buf[mine] = act.astype(bf16)
-
-    for d in (2, 1, SIDE - 1):
-        _, device = first_peer(d)
-        pltpu.make_async_remote_copy(
-            src_ref=act_buf.at[mine],
-            dst_ref=act_buf.at[mine],
-            send_sem=send_sem.at[7],
-            recv_sem=recv_sem.at[7],
-            device_id=device,
-            device_id_type=MESH,
-        ).start()
-    departed(6, piece_in)
-    arrive(7, act_buf, CLASSES - 1)
-    units = jnp.concatenate([act_buf[c] for c in range(CLASSES)], axis=1)
+
+    @pl.when(owns)
+    def own_chunk():
+        chunk_in[seq] = chunk_out[mine_p]
+        chunk_sum[...] = jnp.zeros((REQUESTS, 2 * CHUNK + LANES), f32)
+        arrive(5, chunk_in, DEVICES - 1)
+
+        @pl.loop(0, DEVICES // 8)
+        def add(i):
+            total = chunk_sum[...]
+            for k in range(8):
+                total = total + chunk_in[i * 8 + k].astype(f32)
+            chunk_sum[...] = total
+
+        total = chunk_sum[...]
+        inv_norm = lax.rsqrt(total[:, 2 * CHUNK : 2 * CHUNK + 1] / MODEL_WIDTH + epsilon)
+        gate = total[:, :CHUNK] * inv_norm
+        act = gate / (1.0 + jnp.exp(-gate)) * (total[:, CHUNK : 2 * CHUNK] * inv_norm)
+        act_buf[mine_p] = act.astype(bf16)
+        for dy, dz in NEAR:
+            other = lax.rem(row_y + dy, SIDE) * SIDE + lax.rem(row_z + dz, SIDE)
+            pltpu.make_async_remote_copy(
+                src_ref=act_buf.at[mine_p],
+                dst_ref=act_buf.at[mine_p],
+                send_sem=send_sem.at[6],
+                recv_sem=recv_sem.at[6],
+                device_id=(other, head),
+                device_id_type=MESH,
+            ).start()
+        departed(5, chunk_in, 2 * OWNERS - 1)
+        arrive(6, act_buf, OWNERS - 1)
+
+    @pl.when(jnp.logical_not(owns))
+    def no_chunk():
+        departed(5, chunk_in, 2 * OWNERS)
+        arrive(6, act_buf, OWNERS)
+
+    units = jnp.concatenate([act_buf[p] for p in range(OWNERS)], axis=1)
     down_buf[head] = jnp.dot(units, wdown[...], preferred_element_type=f32)
-    exchange(8, head_peer, lambda o: down_buf.at[head], lambda d: down_buf.at[head])
-    departed(7, act_buf, CLASSES - 1)
-    arrive(8, down_buf)
+    exchange(7, head_peer, lambda o: down_buf.at[head], lambda d: down_buf.at[head])
+
+    @pl.when(owns)
+    def act_sent():
+        departed(6, act_buf, len(NEAR))
+
+    arrive(7, down_buf)
     down = down_buf[0]
     for h in range(1, HEADS):
         down = down + down_buf[h]
     both_ref[...] = jnp.concatenate([after, after + down], axis=0).astype(bf16)
-    departed(8, down_buf)
+    departed(7, down_buf)
 
 
 def on_device(
@@ -438,11 +483,10 @@
             pltpu.VMEM((requests, part_width), bf16),
             pltpu.VMEM((PEERS, requests, part_width), bf16),
             pltpu.VMEM((HEADS, REQUESTS, LANES), f32),
-            pltpu.VMEM((CLASSES, REQUESTS, 2 * CHUNK + LANES), bf16),
-            pltpu.VMEM((PEERS, REQUESTS, 2 * CHUNK + LANES), bf16),
-            pltpu.VMEM((REQUESTS, 2 * CHUNK + LANES), bf16),
-            pltpu.VMEM((PEERS, REQUESTS, 2 * CHUNK + LANES), bf16),
-            pltpu.VMEM((CLASSES, REQUESTS, CHUNK), bf16),
+            pltpu.VMEM((REQUESTS, 2 * CHUNK + LANES), f32),
+            pltpu.VMEM((OWNERS, REQUESTS, 2 * CHUNK + LANES), bf16),
+            pltpu.VMEM((DEVICES, REQUESTS, 2 * CHUNK + LANES), bf16),
+            pltpu.VMEM((DEVICES // 2, REQUESTS, CHUNK), bf16),
             pltpu.VMEM((HEADS, REQUESTS, LANES), f32),
             pltpu.SemaphoreType.DMA((9,)),
             pltpu.SemaphoreType.DMA((9,)),

time: 57.6 us -> 58.3 us (1.012)
  Pallas kernels: 56.3 us -> 56.9 us
    pallas_call x1, Pallas kernels: 56.3 us -> 56.9 us  [on_device(): pl.pallas_call(layer, out_shape=out, in_specs=[hbm_spec] * len(arrays), o...]
where the time goes in v9:
time: 58.3 us; the launch traced here: 58.1 us
  Pallas kernels  56.9 us (98%)
  between operations  0.64 us (1%)
    pallas_call x1, Pallas kernels, on_device(): pl.pallas_call(layer, out_shape=out, in_specs=[hbm_spec] * len(arrays), o...  56.9 us

profile of v9, /device:TPU:1, one launch (start us, length us, event | category | flops | bytes accessed | tf_op | source)
XLA Modules:
  0.0 58.1 jit_solution(657674714906460097)
XLA Ops:
  0.6 56.9 %shard_map.140 = bf16[8,128]{1,0:T(8,128)(2,1)S(1)} custom-call(bf16[4,128]{1,0:T(4,128)(2,1)} %hidden_any.1, bf16[1,128]{1,0:T(2,128)(2,1)} %bitcast.2, bf16[128,1280]{1,0:T(8,128)(2,1)} %wqkv_any.1, bf16[16,128,128]{2,1,0:T(8,128)(2,1)} %keys_any.1, bf16[16,128,128]{2,1,0:T(8,128)(2,1)} %values_any.1, s32[4,256]{1,0:T(4,128)} %table_any.1, ...), custom_call_target="tpu_custom_call" | custom-call | tf_op jit(solution)/shard_map/pallas_call | solution.py:465
  57.5 0.6 fusion

commit v10 on v6

--- a/solution.py
+++ b/solution.py
@@ -80,7 +80,6 @@
     qkv_out2,
     qkv_in2,
     live_buf,
-    keys_turned,
     part_out1,
     part_in1,
     part_out2,
@@ -217,16 +216,7 @@
     qkv_out2[...] = total.astype(bf16)
     exchange(1, second_peer, lambda o: qkv_out2, lambda d: qkv_in2.at[d - 1])
     loads["keys"].wait()
-
-    @pl.loop(0, SLOTS // 4)
-    def turn(step):
-        for k in range(4):
-            j = step * 4 + k
-            span = pl.ds(pl.multiple_of(j * PAGE_TOKENS, PAGE_TOKENS), PAGE_TOKENS)
-            keys_turned[:, span] = keys[j].T
-
     loads["values"].wait()
-    departed(0, qkv_in1)
     arrive(1, qkv_in2)
     for d in range(7):
         total = total + qkv_in2[d].astype(f32)
@@ -245,7 +235,12 @@
 
     scale = 1.0 / math.sqrt(HEAD_SIZE)
     tokens = SLOTS * PAGE_TOKENS
-    scores = jnp.dot(queries, keys_turned[...], preferred_element_type=f32)
+    scores = lax.dot_general(
+        queries,
+        keys[...].reshape(tokens, HEAD_SIZE),
+        (((1,), (1,)), ((), ())),
+        preferred_element_type=f32,
+    )
     live = live_buf[...] > 0.5
     masked = jnp.where(live, scores.reshape(4, 8, tokens) * scale, neg_fill)
     new_score = (
@@ -308,7 +303,6 @@
     exchange(2, first_peer, lambda o: part_out1, lambda d: part_in1.at[d - 1])
     loads["wout"].wait()
     loads["fgain"].wait()
-    departed(1, qkv_in2)
     arrive(2, part_in1)
     means, stats = merged(means, stats, part_in1)
     part_out2[...] = packed(means, stats)
@@ -316,14 +310,12 @@
     loads["wgate"].wait()
     loads["wup"].wait()
     loads["wdown"].wait()
-    departed(2, part_in1)
     arrive(3, part_in2)
     means, _ = merged(means, stats, part_in2)
 
     attention = jnp.concatenate(means, axis=1).astype(bf16)
     proj_buf[head] = jnp.dot(attention, wout[...], preferred_element_type=f32)
     exchange(4, head_peer, lambda o: proj_buf.at[head], lambda d: proj_buf.at[head])
-    departed(3, part_in2)
     arrive(4, proj_buf)
     projected = proj_buf[0]
     for h in range(1, HEADS):
@@ -344,13 +336,11 @@
     )
     mine = lax.rem(first, CLASSES)
     total = chunk_out[mine].astype(f32)
-    departed(4, proj_buf)
     arrive(5, chunk_in)
     for d in range(PEERS):
         total = total + chunk_in[d].astype(f32)
     piece_out[...] = total.astype(bf16)
     exchange(6, second_peer, lambda o: piece_out, lambda d: piece_in.at[d - 1])
-    departed(5, chunk_in)
     arrive(6, piece_in)
     for d in range(PEERS):
         total = total + piece_in[d].astype(f32)
@@ -369,17 +359,23 @@
             device_id=device,
             device_id_type=MESH,
         ).start()
-    departed(6, piece_in)
     arrive(7, act_buf, CLASSES - 1)
     units = jnp.concatenate([act_buf[c] for c in range(CLASSES)], axis=1)
     down_buf[head] = jnp.dot(units, wdown[...], preferred_element_type=f32)
     exchange(8, head_peer, lambda o: down_buf.at[head], lambda d: down_buf.at[head])
-    departed(7, act_buf, CLASSES - 1)
     arrive(8, down_buf)
     down = down_buf[0]
     for h in range(1, HEADS):
         down = down + down_buf[h]
     both_ref[...] = jnp.concatenate([after, after + down], axis=0).astype(bf16)
+    departed(0, qkv_in1)
+    departed(1, qkv_in2)
+    departed(2, part_in1)
+    departed(3, part_in2)
+    departed(4, proj_buf)
+    departed(5, chunk_in)
+    departed(6, piece_in)
+    departed(7, act_buf, CLASSES - 1)
     departed(8, down_buf)
 
 
@@ -432,7 +428,6 @@
             pltpu.VMEM((requests, qkv_width), bf16),
             pltpu.VMEM((PEERS, requests, qkv_width), bf16),
             pltpu.VMEM((8, SLOTS * PAGE_TOKENS), f32),
-            pltpu.VMEM((HEAD_SIZE, SLOTS * PAGE_TOKENS), bf16),
             pltpu.VMEM((requests, part_width), bf16),
             pltpu.VMEM((PEERS, requests, part_width), bf16),
             pltpu.VMEM((requests, part_width), bf16),

time: 57.6 us -> 57.7 us (level)
  no operation moved by 1% of the time
where the time goes in v10:
time: 57.7 us; the launch traced here: 57.6 us
  Pallas kernels  56.3 us (98%)
  between operations  0.64 us (1%)
    pallas_call x1, Pallas kernels, on_device(): pl.pallas_call(layer, out_shape=out, in_specs=[hbm_spec] * len(arrays), o...  56.3 us

profile of v10, /device:TPU:1, one launch (start us, length us, event | category | flops | bytes accessed | tf_op | source)
XLA Modules:
  0.0 57.6 jit_solution(8694220922211362110)
XLA Ops:
  0.6 56.3 %shard_map.140 = bf16[8,128]{1,0:T(8,128)(2,1)S(1)} custom-call(bf16[4,128]{1,0:T(4,128)(2,1)} %hidden_any.1, bf16[1,128]{1,0:T(2,128)(2,1)} %bitcast.2, bf16[128,1280]{1,0:T(8,128)(2,1)} %wqkv_any.1, bf16[16,128,128]{2,1,0:T(8,128)(2,1)} %keys_any.1, bf16[16,128,128]{2,1,0:T(8,128)(2,1)} %values_any.1, s32[4,256]{1,0:T(4,128)} %table_any.1, ...), custom_call_target="tpu_custom_call" | custom-call | tf_op jit(solution)/shard_map/pallas_call | solution.py:416
  57.0 0.6 fusion
